TPU v7x, 128 devices: a whole 4x4x4 slice. The times are simulated.
128 devices in a mesh: lat: 8 (over y, core), lon: 16 (over x, z).
Axes of the slice: x: 4, y: 4, z: 4, core: 2. Of those that a mesh axis runs over, the one named last changes fastest.
Arguments:
- concentration: float32 [8, 128, 256, 128], P(None, 'lat', 'lon'), may hold values from 0.002 to 0.05
- cotangent: float32 [8, 128, 256, 128], P(None, 'lat', 'lon'), may hold values from -6 to 6
- coag_rate: float32 [8, 128, 256], P(None, 'lat', 'lon'), may hold values from 0.1 to 0.5
- weights: float32 [8, 8, 128, 256], P(None, None, 'lat', 'lon'), may hold values from 0 to 1, as said below
- departure: int32 [8, 8, 128, 256], P(None, None, 'lat', 'lon'), may hold values from 0 to 11263, as said below
- send_list: int32 [8, 16, 9, 1024], P('lat', 'lon'), may hold values from 0 to 2047
Outputs:
- adjoint_field: float32 [8, 128, 256, 128], P(None, 'lat', 'lon')
Inputs may be any that keep to these rules, and one draw needn't show every extreme that they name: `departure`: an entry below 2048 names a cell of the arrival cell's own tile that differs from the arrival cell by at most one in level, in latitude row and in longitude column; an entry 2048 + b * 1024 + s names slot s of block b of the arrival cell's device. Block 4 (the device itself) is never named, nor a block whose latitude tile doesn't exist. Every device names all 1024 slots of block 5. The 8 weights of an arrival cell are trilinear weights: products of three fractions or their complements.
All inputs are finite; a program needn't handle non-finite values.
Results may differ from a plain program's by a relative error of at most 0.0003.
Values sent between devices are 32-bit elements; how exact they have to be, the bound alone decides.
A program may use at most 64 MiB of HBM per device.

v0:
```python
import math

import jax
import jax.numpy as jnp
from jax import lax
from jax.sharding import PartitionSpec as P

HIGHEST = lax.Precision.HIGHEST


def from_behind(value, axis, by):
    devices = lax.axis_size(axis)
    pairs = [(i, i + by) for i in range(devices) if 0 <= i + by < devices]
    return lax.ppermute(value, axis, pairs)


def from_behind_2(value, axis, steps):
    count = lax.axis_size(axis)
    pairs = [(source, (source + steps) % count) for source in range(count)]
    return lax.ppermute(value, axis, pairs)


def spectral_tables(bin_count):
    period = 2 * bin_count
    orders = jnp.arange(bin_count, dtype=jnp.int32)[:, None]
    frequency = jnp.arange(period, dtype=jnp.int32)[None, :]
    angles = (orders * frequency % period).astype(jnp.float32) * (2.0 * math.pi / period)
    forward = jnp.concatenate([jnp.cos(angles), -jnp.sin(angles)], axis=1)
    targets = jnp.arange(bin_count, dtype=jnp.int32)[None, :] - 1
    valid_col = targets >= 0
    back_angles = (frequency.T * jnp.maximum(targets, 0) % period).astype(jnp.float32) * (
        2.0 * math.pi / period
    )
    inverse_scale = 0.5 / period
    inverse = jnp.concatenate(
        [
            jnp.where(valid_col, jnp.cos(back_angles), 0.0) * inverse_scale,
            jnp.where(valid_col, -jnp.sin(back_angles), 0.0) * inverse_scale,
        ],
        axis=0,
    )
    return (forward, inverse)


def coagulate(transported, coefficient, forward, inverse):
    spectrum = jnp.dot(transported, forward, precision=HIGHEST)
    half_len = forward.shape[1] // 2
    real_part = spectrum[:, :half_len]
    imag_part = spectrum[:, half_len:]
    squared = jnp.concatenate(
        [real_part * real_part - imag_part * imag_part, 2.0 * real_part * imag_part], axis=1
    )
    gained = jnp.dot(squared, inverse, precision=HIGHEST)
    totals = jnp.sum(transported, axis=1, keepdims=True)
    return transported + coefficient[:, None] * (gained - transported * totals)


def on_device(concentration, cotangent, coag_rate, weights, departure, send_list):
    levels, lat_cells, lon_cells, bin_count = concentration.shape
    cell_count = levels * lat_cells * lon_cells
    block_count = send_list.shape[2]
    capacity = send_list.shape[3]
    slot_total = block_count * capacity
    own_rows = concentration.reshape(cell_count, bin_count)
    slot_cells = send_list.reshape(slot_total)
    outgoing = own_rows[slot_cells].reshape(3, 3, capacity, bin_count)
    lat_groups = []
    for upper in range(3):
        group = outgoing[upper]
        if upper != 1:
            group = from_behind(group, "lat", 1 - upper)
        lat_groups.append(group)
    after_lat = jnp.stack(lat_groups, axis=0)
    lon_groups = []
    for column in range(3):
        group = after_lat[:, column]
        if column != 1:
            group = from_behind_2(group, "lon", 1 - column)
        lon_groups.append(group)
    incoming = jnp.stack(lon_groups, axis=1)
    incoming_flat = incoming.reshape(slot_total, bin_count)
    corner_count = departure.shape[0]
    flat_index = departure.reshape(corner_count, cell_count)
    flat_weight = weights.reshape(corner_count, cell_count)
    lookup_rows = jnp.concatenate([own_rows, incoming_flat], axis=0)
    transported = jnp.zeros((cell_count, bin_count), jnp.float32)
    for corner in range(corner_count):
        transported = transported + flat_weight[corner][:, None] * lookup_rows[flat_index[corner]]
    forward, inverse = spectral_tables(bin_count)
    cell_rate = coag_rate.reshape(cell_count)

    def advance(state_rows):
        return coagulate(state_rows, cell_rate, forward, inverse)

    unused_out, pullback = jax.vjp(advance, transported)
    adjoint_rows = pullback(cotangent.reshape(cell_count, bin_count))[0]
    weighted = (flat_weight[:, :, None] * adjoint_rows[None]).reshape(
        corner_count * cell_count, bin_count
    )
    slot_sums = jax.ops.segment_sum(
        weighted, flat_index.reshape(-1), num_segments=cell_count + slot_total
    )
    local_part = slot_sums[:cell_count]
    outgoing_back = slot_sums[cell_count:].reshape(3, 3, capacity, bin_count)
    lon_back_groups = []
    for column in range(3):
        group = outgoing_back[:, column]
        if column != 1:
            group = from_behind_2(group, "lon", column - 1)
        lon_back_groups.append(group)
    after_lon = jnp.stack(lon_back_groups, axis=1)
    lat_back_groups = []
    for upper in range(3):
        group = after_lon[upper]
        if upper != 1:
            group = from_behind(group, "lat", upper - 1)
        lat_back_groups.append(group)
    returned = jnp.stack(lat_back_groups, axis=0)
    owned_back = jax.ops.segment_sum(
        returned.reshape(slot_total, bin_count), slot_cells, num_segments=cell_count
    )
    adjoint_total = local_part + owned_back
    return adjoint_total.reshape(levels, lat_cells, lon_cells, bin_count)


def solution(mesh):
    in_specs = (
        P(None, "lat", "lon", None),
        P(None, "lat", "lon", None),
        P(None, "lat", "lon"),
        P(None, None, "lat", "lon"),
        P(None, None, "lat", "lon"),
        P("lat", "lon", None, None),
    )
    out_specs = P(None, "lat", "lon", None)
    return jax.shard_map(
        on_device, mesh=mesh, in_specs=in_specs, out_specs=out_specs, check_vma=False
    )
```

profile of v0, /device:TPU:17, one launch (start us, length us, event | category | flops | bytes accessed | tf_op | source)
XLA Modules:
  0.0 427.8 jit_solution(18234029532904775858)
XLA Ops:
  0.8 32.2 %gather_fusion = f32[9216,128]{1,0:T(8,128)} fusion(f32[2048,128]{1,0:T(8,128)} %bitcast.118, s32[9216]{0:T(1024)S(1)} %broadcast_clamp_fusion), kind=kCustom, calls=%fused_computation | custom fusion | bytes 9474048 | tf_op jit(solution)/shard_map/gather | solution.py:66
  33.1 4.4 %fusion.35 = (f32[3072,128]{1,0:T(8,128)}, f32[3072,128]{1,0:T(8,128)S(1)}, f32[3072,128]{1,0:T(8,128)}) fusion(f32[9216,128]{1,0:T(8,128)} %gather_fusion), kind=kLoop, calls=%fused_computation.100 | loop fusion | bytes 9437184 | tf_op jit(solution)/shard_map/slice | solution.py:69
  37.5 2.7 collective-permute-start.1
  40.2 3.0 collective-permute-start
  63.4 6.0 %collective-permute-start.3 = (f32[3,1024,128]{2,1,0:T(8,128)S(1)}, f32[3,1024,128]{2,1,0:T(8,128)S(1)}, u32[]{:S(2)}, u32[]{:S(2)}) collective-permute-start(f32[3,1024,128]{2,1,0:T(8,128)S(1)} %get-tuple-element.16), channel_id=1, source_target_pairs={{0,15},{1,0},{2,1},{3,2},{4,3},{5,4},{6,5},{7,6},{8,7},{9,8},{10,9... | collective-permute-start | bytes 4718600 | tf_op jit(solution)/shard_map/ppermute | solution.py:20
  71.8 29.8 %collective-permute-done.3 = f32[3,1024,128]{2,1,0:T(8,128)S(1)} collective-permute-done((f32[3,1024,128]{2,1,0:T(8,128)S(1)}, f32[3,1024,128]{2,1,0:T(8,128)S(1)}, u32[]{:S(2)}, u32[]{:S(2)}) %collective-permute-start.3) | collective-permute-done | bytes 1572896 | tf_op jit(solution)/shard_map/ppermute | solution.py:20
  101.6 5.2 %collective-permute-done.2 = f32[3,1024,128]{2,1,0:T(8,128)S(1)} collective-permute-done((f32[3,1024,128]{2,1,0:T(8,128)S(1)}, f32[3,1024,128]{2,1,0:T(8,128)S(1)}, u32[]{:S(2)}, u32[]{:S(2)}) %collective-permute-start.2) | collective-permute-done | bytes 1572896 | tf_op jit(solution)/shard_map/ppermute | solution.py:20
  108.5 3.2 pad_maximum_fusion
  111.6 8.1 %gather_fusion.8 = f32[2048,128]{1,0:T(8,128)S(1)} fusion(f32[11264,128]{1,0:T(8,128)} %pad_maximum_fusion, s32[2048]{0:T(1024)S(1)} %copy-done.9), kind=kCustom, calls=%fused_computation.8 | custom fusion | bytes 2105344 | tf_op jit(solution)/shard_map/gather | solution.py:88
  119.8 8.1 %gather_fusion.7 = f32[2048,128]{1,0:T(8,128)S(1)} fusion(f32[11264,128]{1,0:T(8,128)} %pad_maximum_fusion, s32[2048]{0:T(1024)S(1)} %copy-done.10), kind=kCustom, calls=%fused_computation.7 | custom fusion | bytes 2105344 | tf_op jit(solution)/shard_map/gather | solution.py:88
  127.9 8.1 %gather_fusion.6 = f32[2048,128]{1,0:T(8,128)S(1)} fusion(f32[11264,128]{1,0:T(8,128)} %pad_maximum_fusion, s32[2048]{0:T(1024)S(1)} %copy-done.11), kind=kCustom, calls=%fused_computation.6 | custom fusion | bytes 2105344 | tf_op jit(solution)/shard_map/gather | solution.py:88
  136.0 11.0 %gather_fusion.5 = f32[2048,128]{1,0:T(8,128)} fusion(f32[11264,128]{1,0:T(8,128)} %pad_maximum_fusion, s32[2048]{0:T(1024)} %broadcast_clamp_fusion.4), kind=kCustom, calls=%fused_computation.5 | custom fusion | bytes 2105344 | tf_op jit(solution)/shard_map/gather | solution.py:88
  147.0 10.2 %gather_fusion.4 = f32[2048,128]{1,0:T(8,128)} fusion(f32[11264,128]{1,0:T(8,128)} %pad_maximum_fusion, s32[2048]{0:T(1024)S(1)} %copy-done.12), kind=kCustom, calls=%fused_computation.4 | custom fusion | bytes 2105344 | tf_op jit(solution)/shard_map/gather | solution.py:88
  157.2 10.9 %gather_fusion.3 = f32[2048,128]{1,0:T(8,128)} fusion(f32[11264,128]{1,0:T(8,128)} %pad_maximum_fusion, s32[2048]{0:T(1024)} %broadcast_clamp_fusion.6), kind=kCustom, calls=%fused_computation.3 | custom fusion | bytes 2105344 | tf_op jit(solution)/shard_map/gather | solution.py:88
  168.1 10.2 %gather_fusion.2 = f32[2048,128]{1,0:T(8,128)} fusion(f32[11264,128]{1,0:T(8,128)} %pad_maximum_fusion, s32[2048]{0:T(1024)S(1)} %copy-done.13), kind=kCustom, calls=%fused_computation.2 | custom fusion | bytes 2105344 | tf_op jit(solution)/shard_map/gather | solution.py:88
  178.3 10.9 %gather_fusion.1 = f32[2048,128]{1,0:T(8,128)} fusion(f32[11264,128]{1,0:T(8,128)} %pad_maximum_fusion, s32[2048]{0:T(1024)} %broadcast_clamp_fusion.8), kind=kCustom, calls=%fused_computation.1 | custom fusion | bytes 2105344 | tf_op jit(solution)/shard_map/gather | solution.py:88
  189.2 6.0 %multiply_reduce_fusion = f32[8,16,16]{2,1,0:T(8,128)} fusion(f32[8,16,16,128]{3,2,1,0:T(8,128)} %param.7, f32[8,16,16,128]{3,2,1,0:T(8,128)S(1)} %bitcast.123, f32[8,16,16,128]{3,2,1,0:T(8,128)S(1)} %bitcast.124, f32[8,16,16,128]{3,2,1,0:T(8,128)S(1)} %bitcast.125, f32[8,16,16,128]{3,2,1,0:T(8,128)} %bitcast.126, f32[8,16,16,128]{3,2,1,0:T(8,128)} %bitcast.127, ...), kind=kLoop, calls=%fused_computation.36 | loop fusion | flops 4978688 | bytes 9519104 | tf_op jit(solution)/shard_map/transpose(jvp())/reduce_sum | solution.py:55
  196.2 5.1 %fusion.34 = (f32[2048]{0:T(1024)S(1)}, f32[2048,128]{1,0:T(8,128)S(1)}) fusion(f32[2048,128]{1,0:T(8,128)S(1)} %gather_fusion.8, f32[2048]{0:T(1024)} %mul.287, f32[2048,128]{1,0:T(8,128)S(1)} %gather_fusion.7, f32[2048]{0:T(1024)} %mul.284, f32[2048,128]{1,0:T(8,128)S(1)} %gather_fusion.6, f32[2048]{0:T(1024)} %mul.281, f32[2048,128]{1,0:T(8,128)} %gather_fusion.5, ...), kind=kLoop, calls=%fused_computation.99 | loop fusion | flops 4192256 | bytes 9510912 | tf_op jit(solution)/shard_map/jvp()/reduce_sum | solution.py:54
  202.5 3.5 fusion.10
  206.1 3.5 fusion.14
  210.4 3.6 fusion.6
  214.0 4.6 %bitcast_multiply_fusion = f32[16384,128]{1,0:T(8,128)} fusion(f32[2048,128]{1,0:T(8,128)S(1)} %fusion.6, f32[16384]{0:T(1024)S(1)} %copy-done.6), kind=kLoop, calls=%fused_computation.11 | loop fusion | flops 2097152 | bytes 9502720 | tf_op jit(solution)/shard_map/mul | solution.py:97
  218.6 90.7 %scatter_custom_fusion = f32[11264,128]{1,0:T(8,128)} fusion(s32[16384]{0:T(1024)} %reshape.478, f32[16384,128]{1,0:T(8,128)} %bitcast_multiply_fusion, f32[]{:T(128)} %constant.14.clone.1), kind=kCustom, calls=%fused_computation.23 | custom fusion | flops 2097152 | bytes 5767680 | tf_op jit(solution)/shard_map/scatter-add | solution.py:100
  309.3 2.3 slice-done
  312.0 4.8 %collective-permute-start.4 = (f32[3,1024,128]{2,1,0:T(8,128)S(1)}, f32[3,1024,128]{2,1,0:T(8,128)S(1)}, u32[]{:S(2)}, u32[]{:S(2)}) collective-permute-start(f32[3,1024,128]{2,1,0:T(8,128)S(1)} %get-tuple-element.12), channel_id=1, source_target_pairs={{0,15},{1,0},{2,1},{3,2},{4,3},{5,4},{6,5},{7,6},{8,7},{9,8},{10,9... | collective-permute-start | bytes 4718600 | tf_op jit(solution)/shard_map/ppermute | solution.py:20
  316.8 31.8 %collective-permute-done.5 = f32[3,1024,128]{2,1,0:T(8,128)S(1)} collective-permute-done((f32[3,1024,128]{2,1,0:T(8,128)S(1)}, f32[3,1024,128]{2,1,0:T(8,128)S(1)}, u32[]{:S(2)}, u32[]{:S(2)}) %collective-permute-start.5) | collective-permute-done | bytes 1572896 | tf_op jit(solution)/shard_map/ppermute | solution.py:20
  349.3 3.2 collective-permute-start.7
  352.5 4.1 collective-permute-start.6
  356.7 13.2 %collective-permute-done.7 = f32[3,1024,128]{2,1,0:T(8,128)S(1)} collective-permute-done((f32[3,1024,128]{2,1,0:T(8,128)S(1)}, f32[3,1024,128]{2,1,0:T(8,128)S(1)}, u32[]{:S(2)}, u32[]{:S(2)}) %collective-permute-start.7) | collective-permute-done | bytes 1572896 | tf_op jit(solution)/shard_map/ppermute | solution.py:14
  369.9 4.4 %collective-permute-done.6 = f32[3,1024,128]{2,1,0:T(8,128)S(1)} collective-permute-done((f32[3,1024,128]{2,1,0:T(8,128)S(1)}, f32[3,1024,128]{2,1,0:T(8,128)S(1)}, u32[]{:S(2)}, u32[]{:S(2)}) %collective-permute-start.6) | collective-permute-done | bytes 1572896 | tf_op jit(solution)/shard_map/ppermute | solution.py:14
  374.3 2.5 pad_maximum_fusion.4
  376.7 50.1 %scatter_fusion = f32[2048,128]{1,0:T(8,128)S(1)} fusion(f32[2048,128]{1,0:T(8,128)S(1)} %slice-done.1, s32[9216]{0:T(1024)S(1)} %bitcast.139, f32[9216,128]{1,0:T(8,128)} %bitcast.121), kind=kCustom, calls=%fused_computation.10 | custom fusion | flops 1179648 | bytes 14192640 | tf_op jit(solution)/shard_map/scatter-add | solution.py:119
  (93 shorter events, 29.9 us)
Async XLA Ops:
  33.0 11.2 %copy-start.4 = (s32[8,8,16,16]{3,2,1,0:T(8,128)S(1)}, s32[8,8,16,16]{3,2,1,0:T(8,128)}, u32[]{:S(2)}) copy-start(s32[8,8,16,16]{3,2,1,0:T(8,128)} %param.10) | copy-start | bytes 196612
  33.1 13.5 %copy-start.3 = (f32[8,8,16,16]{3,2,1,0:T(8,128)S(1)}, f32[8,8,16,16]{3,2,1,0:T(8,128)}, u32[]{:S(2)}) copy-start(f32[8,8,16,16]{3,2,1,0:T(8,128)} %param.9) | copy-start | bytes 196612
  37.5 12.2 %copy-start.7 = (f32[8,16,16]{2,1,0:T(8,128)S(1)}, f32[8,16,16]{2,1,0:T(8,128)}, u32[]{:S(2)}) copy-start(f32[8,16,16]{2,1,0:T(8,128)} %param.8) | copy-start | bytes 24580
  37.5 22.5 %collective-permute-start.1 = (f32[3,1024,128]{2,1,0:T(8,128)}, f32[3,1024,128]{2,1,0:T(8,128)}, u32[]{:S(2)}, u32[]{:S(2)}) collective-permute-start(f32[3,1024,128]{2,1,0:T(8,128)} %bitcast.7), channel_id=1, source_target_pairs={{16,0},{32,16},{48,32},{64,48},{80,64},{96,80},{112,96},{17,1},{33... | collective-permute-start | bytes 4718600 | tf_op jit(solution)/shard_map/ppermute | solution.py:14
  40.2 20.6 %collective-permute-start = (f32[3,1024,128]{2,1,0:T(8,128)}, f32[3,1024,128]{2,1,0:T(8,128)}, u32[]{:S(2)}, u32[]{:S(2)}) collective-permute-start(f32[3,1024,128]{2,1,0:T(8,128)} %bitcast.4), channel_id=1, source_target_pairs={{0,16},{16,32},{32,48},{48,64},{64,80},{80,96},{96,112},{1,17},{17... | collective-permute-start | bytes 4718600 | tf_op jit(solution)/shard_map/ppermute | solution.py:14
  63.0 7.6 %copy-start.14 = (s32[128]{0:T(128)S(1)}, s32[128]{0:T(128)}, u32[]{:S(2)}) copy-start(s32[128]{0:T(128)} %fusion.28) | copy-start | bytes 1540
  63.0 7.6 %copy-start.15 = (pred[128]{0:T(512)(128)(4,1)S(1)}, pred[128]{0:T(512)(128)(4,1)}, u32[]{:S(2)}) copy-start(pred[128]{0:T(512)(128)(4,1)} %fusion.29) | copy-start | bytes 388
  63.4 38.3 %collective-permute-start.3 = (f32[3,1024,128]{2,1,0:T(8,128)S(1)}, f32[3,1024,128]{2,1,0:T(8,128)S(1)}, u32[]{:S(2)}, u32[]{:S(2)}) collective-permute-start(f32[3,1024,128]{2,1,0:T(8,128)S(1)} %get-tuple-element.16), channel_id=1, source_target_pairs={{0,15},{1,0},{2,1},{3,2},{4,3},{5,4},{6,5},{7,6},{8,7},{9,8},{10,9... | collective-permute-start | bytes 4718600 | tf_op jit(solution)/shard_map/ppermute | solution.py:20
  69.4 37.5 %collective-permute-start.2 = (f32[3,1024,128]{2,1,0:T(8,128)S(1)}, f32[3,1024,128]{2,1,0:T(8,128)S(1)}, u32[]{:S(2)}, u32[]{:S(2)}) collective-permute-start(f32[3,1024,128]{2,1,0:T(8,128)S(1)} %get-tuple-element.15), channel_id=1, source_target_pairs={{0,1},{1,2},{2,3},{3,4},{4,5},{5,6},{6,7},{7,8},{8,9},{9,10},{10,1... | collective-permute-start | bytes 4718600 | tf_op jit(solution)/shard_map/ppermute | solution.py:20
  107.2 1.2 copy-start
  108.5 3.2 copy-start.9
  111.6 8.1 %copy-start.10 = (s32[2048]{0:T(1024)S(1)}, s32[2048]{0:T(1024)}, u32[]{:S(2)}) copy-start(s32[2048]{0:T(1024)} %broadcast_clamp_fusion.2) | copy-start | bytes 24580
  119.8 8.1 %copy-start.11 = (s32[2048]{0:T(1024)S(1)}, s32[2048]{0:T(1024)}, u32[]{:S(2)}) copy-start(s32[2048]{0:T(1024)} %broadcast_clamp_fusion.3) | copy-start | bytes 24580
  136.0 11.0 %copy-start.12 = (s32[2048]{0:T(1024)S(1)}, s32[2048]{0:T(1024)}, u32[]{:S(2)}) copy-start(s32[2048]{0:T(1024)} %broadcast_clamp_fusion.5) | copy-start | bytes 24580
  157.2 10.9 %copy-start.13 = (s32[2048]{0:T(1024)S(1)}, s32[2048]{0:T(1024)}, u32[]{:S(2)}) copy-start(s32[2048]{0:T(1024)} %broadcast_clamp_fusion.7) | copy-start | bytes 24580
  196.1 5.1 %copy-start.2 = (f32[8,16,16,128]{3,2,1,0:T(8,128)S(1)}, f32[8,16,16,128]{3,2,1,0:T(8,128)}, u32[]{:S(2)}) copy-start(f32[8,16,16,128]{3,2,1,0:T(8,128)} %param.7) | copy-start | bytes 3145732
  196.1 6.4 %copy-start.5 = (f32[256,128]{1,0:T(8,128)S(1)}, f32[256,128]{1,0:T(8,128)}, u32[]{:S(2)}) copy-start(f32[256,128]{1,0:T(8,128)} %get-tuple-element.48) | copy-start | bytes 393220
  210.3 3.6 copy-start.6
  309.3 2.3 slice-start
  311.9 36.6 %collective-permute-start.5 = (f32[3,1024,128]{2,1,0:T(8,128)S(1)}, f32[3,1024,128]{2,1,0:T(8,128)S(1)}, u32[]{:S(2)}, u32[]{:S(2)}) collective-permute-start(f32[3,1024,128]{2,1,0:T(8,128)S(1)} %get-tuple-element.13), channel_id=1, source_target_pairs={{0,1},{1,2},{2,3},{3,4},{4,5},{5,6},{6,7},{7,8},{8,9},{9,10},{10,1... | collective-permute-start | bytes 4718600 | tf_op jit(solution)/shard_map/ppermute | solution.py:20
  312.0 36.6 %collective-permute-start.4 = (f32[3,1024,128]{2,1,0:T(8,128)S(1)}, f32[3,1024,128]{2,1,0:T(8,128)S(1)}, u32[]{:S(2)}, u32[]{:S(2)}) collective-permute-start(f32[3,1024,128]{2,1,0:T(8,128)S(1)} %get-tuple-element.12), channel_id=1, source_target_pairs={{0,15},{1,0},{2,1},{3,2},{4,3},{5,4},{6,5},{7,6},{8,7},{9,8},{10,9... | collective-permute-start | bytes 4718600 | tf_op jit(solution)/shard_map/ppermute | solution.py:20
  349.3 20.6 %collective-permute-start.7 = (f32[3,1024,128]{2,1,0:T(8,128)S(1)}, f32[3,1024,128]{2,1,0:T(8,128)S(1)}, u32[]{:S(2)}, u32[]{:S(2)}) collective-permute-start(f32[3,1024,128]{2,1,0:T(8,128)S(1)} %get-tuple-element.10), channel_id=1, source_target_pairs={{0,16},{16,32},{32,48},{48,64},{64,80},{80,96},{96,112},{1,17},{17... | collective-permute-start | bytes 4718600 | tf_op jit(solution)/shard_map/ppermute | solution.py:14
  352.5 21.7 %collective-permute-start.6 = (f32[3,1024,128]{2,1,0:T(8,128)S(1)}, f32[3,1024,128]{2,1,0:T(8,128)S(1)}, u32[]{:S(2)}, u32[]{:S(2)}) collective-permute-start(f32[3,1024,128]{2,1,0:T(8,128)S(1)} %get-tuple-element.9), channel_id=1, source_target_pairs={{16,0},{32,16},{48,32},{64,48},{80,64},{96,80},{112,96},{17,1},{33... | collective-permute-start | bytes 4718600 | tf_op jit(solution)/shard_map/ppermute | solution.py:14
  374.2 2.5 slice-start.1
  374.2 2.5 copy-start.8
  426.9 1.0 copy-start.1
where the time goes:
time: 434 us; the launch traced here: 428 us
  other arithmetic  176 us (41%)
  local copies, waits for them, and re-layouts  132 us (30%)
  waiting for transfers between devices  85.4 us (20%)
  starting transfers between devices  23.9 us (6%)
  matrix products  10.7 us (2%)
    scatter-add x1, other arithmetic, on_device(): jax.ops.segment_sum(weighted, flat_index.reshape(-1), num_segments=cell_c...  90.7 us
    gather x8, local copies, waits for them, and re-layouts, on_device(): lookup_rows[flat_index[corner]]  77.5 us
    ppermute x4, waiting for transfers between devices, from_behind_2(): return lax.ppermute(value, axis, pairs)  66.9 us
    scatter-add x1, other arithmetic, on_device(): jax.ops.segment_sum(returned.reshape(slot_total, bin_count), slot_cells,...  50.1 us
    gather x1, local copies, waits for them, and re-layouts, on_device(): outgoing = own_rows[slot_cells].reshape(3, 3, capacity, bin_count)  32.2 us
    ppermute x4, waiting for transfers between devices, from_behind(): return lax.ppermute(value, axis, pairs)  18.5 us
    ppermute x4, starting transfers between devices, from_behind(): return lax.ppermute(value, axis, pairs)  13.1 us
    ppermute x4, starting transfers between devices, from_behind_2(): return lax.ppermute(value, axis, pairs)  10.9 us
  transfers between devices with their start and end apart: 8, of which 7 were waited for; matrix products, arithmetic and copies ran while one was open for 4% of the time, Pallas kernels for 0%

commit v1 on v0

v1 whole, which is shorter than its diff:
```python
import functools

import jax
import jax.numpy as jnp
import numpy as np
from jax import lax
from jax.experimental import pallas as pl
from jax.experimental.pallas import tpu as pltpu
from jax.sharding import PartitionSpec as P

MESH = pl.DeviceIdType.MESH
F32 = jnp.float32
BF16 = jnp.bfloat16
I16 = jnp.int16
I32 = jnp.int32
SMEM = pl.BlockSpec(memory_space=pltpu.SMEM)
VMEM = pl.BlockSpec(memory_space=pltpu.VMEM)
ANY = pl.BlockSpec(memory_space=pl.ANY)
ORDER = ((0, 0), (2, 2), (0, 2), (2, 0), (1, 0), (1, 2), (0, 1), (2, 1))
ACCS = 4


def split(x):
    hi = x.astype(BF16)
    return hi, (x - hi.astype(F32)).astype(BF16)


def spectral_tables(bins):
    period = 2 * bins
    k = np.arange(bins)
    n = np.arange(bins)[:, None]
    angle = 2.0 * np.pi * (n * k % period) / period
    sine = -np.sin(angle)
    sine[:, 0] = np.cos(np.pi * np.arange(bins))
    forward = np.concatenate([np.cos(angle), sine], axis=1)
    lag = np.arange(1, bins + 1)[None, :]
    back = 2.0 * np.pi * (k[:, None] * lag % period) / period
    scale = np.where(k == 0, 1.0, 2.0)[:, None] / period
    real = np.cos(back) * scale
    imag = -np.sin(back) * scale
    imag[0] = np.cos(np.pi * lag[0]) / period
    inverse = np.concatenate([real, imag], axis=0)
    return forward.astype(np.float32), inverse.astype(np.float32)


class Place:
    def __init__(self, n_lat, n_lon):
        self.lat = lax.axis_index("lat")
        self.lon = lax.axis_index("lon")
        self.n_lat = n_lat
        self.n_lon = n_lon

    def has(self, u):
        there = self.lat + u - 1
        return (there >= 0) & (there < self.n_lat)

    def at(self, u, v):
        return (self.lat + u - 1, lax.rem(self.lon + v - 1 + self.n_lon, self.n_lon))

    def greet(self):
        barrier = pltpu.get_barrier_semaphore()
        for u, v in ORDER:
            @pl.when(self.has(u))
            def _():
                pl.semaphore_signal(barrier, inc=1, device_id=self.at(u, v), device_id_type=MESH)
        count = jnp.where(self.lat > 0, 3, 0) + jnp.where(self.lat < self.n_lat - 1, 3, 0) + 2
        pl.semaphore_wait(barrier, count)


def send_kernel(n_lat, n_lon, cells, cap, slots, own, table, rows, own_sem, send_sem, recv_sem):
    place = Place(n_lat, n_lon)
    place.greet()
    keep = pltpu.make_async_copy(own, table.at[pl.ds(0, cells)], own_sem)
    keep.start()

    def copy(u, v):
        b = 3 * u + v
        return pltpu.make_async_remote_copy(
            src_ref=rows.at[b], dst_ref=table.at[pl.ds(cells + b * cap, cap)], send_sem=send_sem.at[b],
            recv_sem=recv_sem.at[b], device_id=place.at(2 - u, 2 - v), device_id_type=MESH)

    for u, v in ORDER:
        @pl.when(place.has(2 - u))
        def _():
            b = 3 * u + v
            step = 32

            def gather(i, carry):
                for j in range(step):
                    s = i * step + j
                    rows[b, pl.ds(s, 1), :] = own[pl.ds(slots[b * cap + s], 1), :]
                return carry

            lax.fori_loop(0, cap // step, gather, 0)
            copy(u, v).start()
    keep.wait()
    for u, v in ORDER:
        @pl.when(place.has(u))
        def _():
            copy(u, v).wait_recv()

        @pl.when(place.has(2 - u))
        def _():
            copy(u, v).wait_send()


def cell_kernel(cells, corners, index, weight, table, cot, rate, fwd_hi, fwd_lo, inv_hi, inv_lo, out, state, *more):
    accs = (out,) + more
    step = 4

    def gather(i, carry):
        for j in range(step):
            a = i * step + j
            total = None
            for k in range(corners):
                row = table[pl.ds(index[k * cells + a], 1), :] * weight[k * cells + a]
                total = row if total is None else total + row
            state[pl.ds(a, 1), :] = total
        return carry

    lax.fori_loop(0, cells // step, gather, 0)
    tile = 256
    bins = cot.shape[1]
    first = lax.broadcasted_iota(I32, (tile, bins), 1) == 0

    def dot3(x, hi, lo):
        xh, xl = split(x)
        out = jnp.dot(xh, hi[...], preferred_element_type=F32)
        out += jnp.dot(xl, hi[...], preferred_element_type=F32)
        return out + jnp.dot(xh, lo[...], preferred_element_type=F32)

    def react(i, carry):
        here = pl.ds(pl.multiple_of(i * tile, tile), tile)
        t = state[here, :]
        c = cot[here, :]
        ts = dot3(t, fwd_hi, fwd_lo)
        cs = dot3(c, fwd_hi, fwd_lo)
        ta, tb, ca, cb = ts[:, :bins], ts[:, bins:], cs[:, :bins], cs[:, bins:]
        both = tb * cb
        real = ta * ca + jnp.where(first, 0.0, both)
        imag = jnp.where(first, both, ta * cb - tb * ca)
        lagged = dot3(jnp.concatenate([real, imag], axis=1), inv_hi, inv_lo)
        totals = jnp.sum(t, axis=1, keepdims=True)
        weighed = jnp.sum(t * c, axis=1, keepdims=True)
        state[here, :] = c + rate[here, :] * (lagged - totals * c - weighed)
        return carry

    lax.fori_loop(0, cells // tile, react, 0)
    chunk = 512
    for acc in accs:
        def clear(i, carry):
            acc[pl.ds(pl.multiple_of(i * chunk, chunk), chunk), :] = jnp.zeros((chunk, bins), F32)
            return carry

        lax.fori_loop(0, out.shape[0] // chunk, clear, 0)
    step = 2

    def scatter(i, carry):
        for j in range(step):
            a = i * step + j
            row = state[pl.ds(a, 1), :]
            for k in range(0, corners, ACCS):
                at = [pl.ds(index[(k + m) * cells + a], 1) for m in range(ACCS)]
                new = [accs[m][at[m], :] + row * weight[(k + m) * cells + a] for m in range(ACCS)]
                for m in range(ACCS):
                    accs[m][at[m], :] = new[m]
        return carry

    lax.fori_loop(0, cells // step, scatter, 0)

    def merge(i, carry):
        here = pl.ds(pl.multiple_of(i * chunk, chunk), chunk)
        total = out[here, :]
        for acc in more:
            total = total + acc[here, :]
        out[here, :] = total
        return carry

    lax.fori_loop(0, out.shape[0] // chunk, merge, 0)


def return_kernel(n_lat, n_lon, cells, cap, slots, sums, out, back, send_sem, recv_sem):
    place = Place(n_lat, n_lon)
    place.greet()

    def copy(u, v):
        b = 3 * u + v
        return pltpu.make_async_remote_copy(
            src_ref=sums.at[pl.ds(cells + b * cap, cap)], dst_ref=back.at[b], send_sem=send_sem.at[b],
            recv_sem=recv_sem.at[b], device_id=place.at(u, v), device_id_type=MESH)

    for u, v in ORDER:
        @pl.when(place.has(u))
        def _():
            copy(u, v).start()
    out[...] = sums[pl.ds(0, cells), :]
    tile = 256
    bins = out.shape[1]
    number = lax.broadcasted_iota(I32, (tile, cap), 0).astype(I16)
    for u, v in ORDER[6:] + ORDER[:6]:
        @pl.when(place.has(2 - u))
        def _():
            b = 3 * u + v
            copy(u, v).wait_recv()
            rows = jnp.concatenate(split(back[b]), axis=1)
            named = slots[pl.ds(b, 1), :]

            def add(i, carry):
                here = pl.ds(pl.multiple_of(i * tile, tile), tile)
                hit = (named - i * tile).astype(I16) == number
                pick = jnp.where(hit, jnp.ones((), BF16), jnp.zeros((), BF16))
                got = jnp.dot(pick, rows, preferred_element_type=F32)
                out[here, :] += got[:, :bins] + got[:, bins:]
                return carry

            lax.fori_loop(0, cells // tile, add, 0)
    for u, v in ORDER:
        @pl.when(place.has(u))
        def _():
            copy(u, v).wait_send()


def on_device(n_lat, n_lon, concentration, cotangent, coag_rate, weights, departure, send_list):
    levels, lat_cells, lon_cells, bins = concentration.shape
    cells = levels * lat_cells * lon_cells
    blocks, cap = send_list.shape[2:]
    corners = departure.shape[0]
    entries = cells + blocks * cap
    own = concentration.reshape(cells, bins)
    dma = pltpu.SemaphoreType.DMA
    table = pl.pallas_call(
        functools.partial(send_kernel, n_lat, n_lon, cells, cap),
        out_shape=jax.ShapeDtypeStruct((entries, bins), F32),
        in_specs=[SMEM, VMEM], out_specs=ANY,
        scratch_shapes=[pltpu.VMEM((blocks, cap, bins), F32), dma, dma((blocks,)), dma((blocks,))],
        compiler_params=pltpu.CompilerParams(
            collective_id=0, has_side_effects=True, vmem_limit_bytes=16 * 2**20),
    )(send_list.reshape(blocks * cap), own)
    forward, inverse = spectral_tables(bins)
    fwd_hi, fwd_lo = split(jnp.asarray(forward))
    inv_hi, inv_lo = split(jnp.asarray(inverse))
    sums = pl.pallas_call(
        functools.partial(cell_kernel, cells, corners),
        out_shape=jax.ShapeDtypeStruct((entries, bins), F32),
        in_specs=[SMEM, SMEM] + [VMEM] * 7, out_specs=VMEM,
        scratch_shapes=[pltpu.VMEM((cells, bins), F32)] + [pltpu.VMEM((entries, bins), F32)] * (ACCS - 1),
        compiler_params=pltpu.CompilerParams(vmem_limit_bytes=48 * 2**20),
    )(departure.reshape(-1), weights.reshape(-1), table, cotangent.reshape(cells, bins),
      coag_rate.reshape(cells, 1), fwd_hi, fwd_lo, inv_hi, inv_lo)
    total = pl.pallas_call(
        functools.partial(return_kernel, n_lat, n_lon, cells, cap),
        out_shape=jax.ShapeDtypeStruct((cells, bins), F32),
        in_specs=[VMEM, VMEM], out_specs=VMEM,
        scratch_shapes=[pltpu.VMEM((blocks, cap, bins), F32), dma((blocks,)), dma((blocks,))],
        compiler_params=pltpu.CompilerParams(
            collective_id=1, has_side_effects=True, vmem_limit_bytes=32 * 2**20),
    )(send_list.reshape(blocks, cap), sums)
    return total.reshape(levels, lat_cells, lon_cells, bins)


def solution(mesh):
    grid = P(None, "lat", "lon", None)
    field = P(None, "lat", "lon")
    corner = P(None, None, "lat", "lon")
    lists = P("lat", "lon", None, None)
    body = functools.partial(on_device, mesh.shape["lat"], mesh.shape["lon"])
    return jax.shard_map(
        body, mesh=mesh, in_specs=(grid, grid, field, corner, corner, lists), out_specs=grid, check_vma=False)
```

time: 434 us -> 164 us (0.38)
  other arithmetic: 176 us -> 0 us
  Pallas kernels: 0 us -> 152 us
  local copies, waits for them, and re-layouts: 132 us -> 9.06 us
  waiting for transfers between devices: 85.4 us -> 0 us
  starting transfers between devices: 23.9 us -> 0 us
  matrix products: 10.7 us -> 0 us
    pallas_call x0 -> x3, Pallas kernels: none -> 152 us  [the longest x1 59.3 us: on_device(): pl.pallas_call(functools.partial(cell_kernel, cells, corners), out_shape=...]
    scatter-add x2 -> x0, other arithmetic: 141 us -> none  [the longest x1 90.7 us: on_device(): jax.ops.segment_sum(weighted, flat_index.reshape(-1), num_segments=cell_c...]
    gather x9 -> x0, local copies, waits for them, and re-layouts: 110 us -> none  [the longest x8 77.5 us: on_device(): lookup_rows[flat_index[corner]]]
    ppermute x8 -> x0, waiting for transfers between devices: 85.4 us -> none  [the longest x4 66.9 us: from_behind_2(): return lax.ppermute(value, axis, pairs)]
    ppermute x8 -> x0, starting transfers between devices: 23.9 us -> none  [the longest x4 13.1 us: from_behind(): return lax.ppermute(value, axis, pairs)]
    reduce_sum x2 -> x0, other arithmetic: 11.1 us -> none  [the longest x1 5.98 us: coagulate(): return transported + coefficient[:, None] * (gained - transported * totals)]
    dot_general x3 -> x0, matrix products: 10.7 us -> none  [the longest x2 7.12 us: coagulate(): spectrum = jnp.dot(transported, forward, precision=HIGHEST)]
    mul x10 -> x0, local copies, waits for them, and re-layouts: 8.82 us -> none  [the longest x8 7.94 us: on_device(): flat_weight[corner][:, None] * lookup_rows[flat_index[corner]]]
  transfers between devices with their start and end apart: 8 -> 0, of which waited for: 7 -> 0; matrix products, arithmetic and copies ran while one was open for 4% -> 0% of each run, Pallas kernels for 0% -> 0%
where the time goes in v1:
time: 164 us; the launch traced here: 162 us
  Pallas kernels  152 us (93%)
  local copies, waits for them, and re-layouts  9.06 us (6%)
    pallas_call x1, Pallas kernels, on_device(): pl.pallas_call(functools.partial(cell_kernel, cells, corners), out_shape=...  59.3 us
    pallas_call x1, Pallas kernels, on_device(): pl.pallas_call(functools.partial(send_kernel, n_lat, n_lon, cells, cap),...  47.5 us
    pallas_call x1, Pallas kernels, on_device(): pl.pallas_call(functools.partial(return_kernel, n_lat, n_lon, cells, cap)...  45.5 us
    unnamed x28, local copies, waits for them, and re-layouts  8.11 us

profile of v1, /device:TPU:17, one launch (start us, length us, event | category | flops | bytes accessed | tf_op | source)
XLA Modules:
  0.0 161.5 jit_solution(5850581264972576467)
XLA Ops:
  0.0 0.0 copy-start.2
  0.0 1.2 copy-done.2
  1.2 0.0 copy-start.4
  1.2 0.8 copy-done.4
  2.0 0.0 copy-start.12
  2.0 0.0 copy-start.10
  2.0 0.0 copy-start.11
  2.0 0.0 copy-start.6
  2.0 0.0 copy-start.7
  2.0 0.0 copy-start.8
  2.0 0.0 copy-start.9
  2.1 47.5 %shard_map.82.table = f32[11264,128]{1,0:T(8,128)S(1)} custom-call(s32[9216]{0:T(1024)S(1)} %bitcast.15, f32[2048,128]{1,0:T(8,128)S(1)} %bitcast.12), custom_call_target="tpu_custom_call" | custom-call | tf_op jit(solution)/shard_map/pallas_call | solution.py:231
  49.6 0.0 copy-start.1
  49.6 2.5 %copy-done.1 = f32[11264,128]{1,0:T(8,128)} copy-done((f32[11264,128]{1,0:T(8,128)}, f32[11264,128]{1,0:T(8,128)S(1)}, u32[]{:S(2)}) %copy-start.1) | copy-done | bytes 5767192
  52.1 0.0 copy-done.12
  52.1 0.6 reshape.32.rate
  52.6 0.0 copy-done.10
  52.6 0.2 reshape.25.index
  52.8 0.0 copy-done.11
  52.8 0.2 reshape.26.weight
  53.0 0.0 copy-done.3
  53.1 0.0 copy-done.6
  53.1 0.0 copy-done.7
  53.1 0.0 copy-done.8
  53.1 0.0 copy-done.9
  53.1 0.0 copy-start.5
  53.1 59.3 %shard_map.83.sums = f32[11264,128]{1,0:T(8,128)} custom-call(s32[16384]{0:T(1024)S(1)} %reshape.25.index, f32[16384]{0:T(1024)S(1)} %reshape.26.weight, f32[11264,128]{1,0:T(8,128)} %copy-done.1, f32[2048,128]{1,0:T(8,128)S(1)} %bitcast.13, f32[2048,1]{1,0:T(8,128)S(1)} %reshape.32.rate, bf16[128,256]{1,0:T(8,128)(2,1)S(1)} %copy-done.9, ...), custom_call_target="tpu_custom_call" | custom-call | tf_op jit(solution)/shard_map/pallas_call | solution.py:242
  112.4 0.0 copy-done.5
  112.5 0.0 copy-start
  112.5 2.6 %copy-done = f32[11264,128]{1,0:T(8,128)S(1)} copy-done((f32[11264,128]{1,0:T(8,128)S(1)}, f32[11264,128]{1,0:T(8,128)}, u32[]{:S(2)}) %copy-start) | copy-done | bytes 5767192
  115.1 45.5 %shard_map.84 = f32[2048,128]{1,0:T(8,128)S(1)} custom-call(s32[9,1024]{1,0:T(8,128)S(1)} %bitcast.14, f32[11264,128]{1,0:T(8,128)S(1)} %copy-done), custom_call_target="tpu_custom_call" | custom-call | tf_op jit(solution)/shard_map/pallas_call | solution.py:250
  160.6 1.0 copy.14
  (2 shorter events, 0.0 us)
Async XLA Ops:
  0.0 1.2 copy-start.2
  1.2 0.8 copy-start.4
  2.0 50.1 %copy-start.12 = (f32[8,16,16]{2,1,0:T(8,128)S(1)}, f32[8,16,16]{2,1,0:T(8,128)}, u32[]{:S(2)}) copy-start(f32[8,16,16]{2,1,0:T(8,128)} %param.10) | copy-start | bytes 24580
  2.0 50.6 %copy-start.10 = (s32[8,8,16,16]{3,2,1,0:T(8,128)S(1)}, s32[8,8,16,16]{3,2,1,0:T(8,128)}, u32[]{:S(2)}) copy-start(s32[8,8,16,16]{3,2,1,0:T(8,128)} %param.12) | copy-start | bytes 196612
  2.0 50.8 %copy-start.11 = (f32[8,8,16,16]{3,2,1,0:T(8,128)S(1)}, f32[8,8,16,16]{3,2,1,0:T(8,128)}, u32[]{:S(2)}) copy-start(f32[8,8,16,16]{3,2,1,0:T(8,128)} %param.11) | copy-start | bytes 196612
  2.0 51.0 %copy-start.3 = (f32[8,16,16,128]{3,2,1,0:T(8,128)S(1)}, f32[8,16,16,128]{3,2,1,0:T(8,128)}, u32[]{:S(2)}) copy-start(f32[8,16,16,128]{3,2,1,0:T(8,128)} %param.9) | copy-start | bytes 3145732
  2.0 51.0 %copy-start.6 = (bf16[128,256]{1,0:T(8,128)(2,1)S(1)}, bf16[128,256]{1,0:T(8,128)(2,1)}, u32[]{:S(2)}) copy-start(bf16[128,256]{1,0:T(8,128)(2,1)} %constant.10.fwd_lo) | copy-start | bytes 196612
  2.0 51.0 %copy-start.7 = (bf16[256,128]{1,0:T(8,128)(2,1)S(1)}, bf16[256,128]{1,0:T(8,128)(2,1)}, u32[]{:S(2)}) copy-start(bf16[256,128]{1,0:T(8,128)(2,1)} %constant.11.inv_hi) | copy-start | bytes 196612
  2.0 51.0 %copy-start.8 = (bf16[256,128]{1,0:T(8,128)(2,1)S(1)}, bf16[256,128]{1,0:T(8,128)(2,1)}, u32[]{:S(2)}) copy-start(bf16[256,128]{1,0:T(8,128)(2,1)} %constant.14.inv_lo) | copy-start | bytes 196612
  2.0 51.0 %copy-start.9 = (bf16[128,256]{1,0:T(8,128)(2,1)S(1)}, bf16[128,256]{1,0:T(8,128)(2,1)}, u32[]{:S(2)}) copy-start(bf16[128,256]{1,0:T(8,128)(2,1)} %constant.7.fwd_hi) | copy-start | bytes 196612
  49.6 2.5 %copy-start.1 = (f32[11264,128]{1,0:T(8,128)}, f32[11264,128]{1,0:T(8,128)S(1)}, u32[]{:S(2)}) copy-start(f32[11264,128]{1,0:T(8,128)S(1)} %shard_map.82.table) | copy-start | bytes 17301508
  53.1 59.3 %copy-start.5 = (s32[1,1,9,1024]{3,1,2,0:T(1,128)S(1)}, s32[1,1,9,1024]{3,1,2,0:T(1,128)}, u32[]{:S(2)}) copy-start(s32[1,1,9,1024]{3,1,2,0:T(1,128)} %param.13) | copy-start | bytes 110596
  112.5 2.6 %copy-start = (f32[11264,128]{1,0:T(8,128)S(1)}, f32[11264,128]{1,0:T(8,128)}, u32[]{:S(2)}) copy-start(f32[11264,128]{1,0:T(8,128)} %shard_map.83.sums) | copy-start | bytes 17301508

commit v2 on v1

--- a/solution.py
+++ b/solution.py
@@ -17,7 +17,9 @@
 VMEM = pl.BlockSpec(memory_space=pltpu.VMEM)
 ANY = pl.BlockSpec(memory_space=pl.ANY)
 ORDER = ((0, 0), (2, 2), (0, 2), (2, 0), (1, 0), (1, 2), (0, 1), (2, 1))
-ACCS = 4
+ROW_BITS = 14
+ROW_MASK = 2**ROW_BITS - 1
+WORD_UNIT = 2.0**-31
 
 
 def split(x):
@@ -43,6 +45,11 @@
     return forward.astype(np.float32), inverse.astype(np.float32)
 
 
+def slot(u, v):
+    b = 3 * u + v
+    return b - (b > 4)
+
+
 class Place:
     def __init__(self, n_lat, n_lon):
         self.lat = lax.axis_index("lat")
@@ -76,7 +83,7 @@
     def copy(u, v):
         b = 3 * u + v
         return pltpu.make_async_remote_copy(
-            src_ref=rows.at[b], dst_ref=table.at[pl.ds(cells + b * cap, cap)], send_sem=send_sem.at[b],
+            src_ref=rows.at[b], dst_ref=table.at[pl.ds(cells + slot(u, v) * cap, cap)], send_sem=send_sem.at[b],
             recv_sem=recv_sem.at[b], device_id=place.at(2 - u, 2 - v), device_id_type=MESH)
 
     for u, v in ORDER:
@@ -104,8 +111,28 @@
             copy(u, v).wait_send()
 
 
-def cell_kernel(cells, corners, index, weight, table, cot, rate, fwd_hi, fwd_lo, inv_hi, inv_lo, out, state, *more):
-    accs = (out,) + more
+def cell_kernel(cells, corners, *refs):
+    (words, table_hbm, cot, rate, fwd_hi, fwd_lo, inv_hi, inv_lo, sums), refs = refs[:9], refs[9:]
+    table, state, refs = refs[0], refs[1], refs[2:]
+    accs, refs = refs[:corners], refs[corners:]
+    word, (word_sem, table_sem, out_sem) = refs[:corners], refs[corners:]
+    entries, bins = table.shape
+    load = pltpu.make_async_copy(table_hbm, table, table_sem)
+    load.start()
+    loads = [pltpu.make_async_copy(words.at[pl.ds(k * cells, cells)], word[k], word_sem.at[k]) for k in range(corners)]
+    for copy in loads:
+        copy.start()
+    chunk = 512
+
+    def clear(i, carry):
+        for acc in accs:
+            acc[pl.ds(pl.multiple_of(i * chunk, chunk), chunk), :] = jnp.zeros((chunk, bins), F32)
+        return carry
+
+    lax.fori_loop(0, entries // chunk, clear, 0)
+    for copy in loads:
+        copy.wait()
+    load.wait()
     step = 4
 
     def gather(i, carry):
@@ -113,14 +140,14 @@
             a = i * step + j
             total = None
             for k in range(corners):
-                row = table[pl.ds(index[k * cells + a], 1), :] * weight[k * cells + a]
+                code = word[k][a]
+                row = table[pl.ds(code & ROW_MASK, 1), :] * jnp.full((1, bins), code, I32).astype(F32)
                 total = row if total is None else total + row
             state[pl.ds(a, 1), :] = total
         return carry
 
     lax.fori_loop(0, cells // step, gather, 0)
     tile = 256
-    bins = cot.shape[1]
     first = lax.broadcasted_iota(I32, (tile, bins), 1) == 0
 
     def dot3(x, hi, lo):
@@ -131,7 +158,7 @@
 
     def react(i, carry):
         here = pl.ds(pl.multiple_of(i * tile, tile), tile)
-        t = state[here, :]
+        t = state[here, :] * WORD_UNIT
         c = cot[here, :]
         ts = dot3(t, fwd_hi, fwd_lo)
         cs = dot3(c, fwd_hi, fwd_lo)
@@ -142,58 +169,55 @@
         lagged = dot3(jnp.concatenate([real, imag], axis=1), inv_hi, inv_lo)
         totals = jnp.sum(t, axis=1, keepdims=True)
         weighed = jnp.sum(t * c, axis=1, keepdims=True)
-        state[here, :] = c + rate[here, :] * (lagged - totals * c - weighed)
+        state[here, :] = (c + rate[here, :] * (lagged - totals * c - weighed)) * WORD_UNIT
         return carry
 
     lax.fori_loop(0, cells // tile, react, 0)
-    chunk = 512
-    for acc in accs:
-        def clear(i, carry):
-            acc[pl.ds(pl.multiple_of(i * chunk, chunk), chunk), :] = jnp.zeros((chunk, bins), F32)
-            return carry
-
-        lax.fori_loop(0, out.shape[0] // chunk, clear, 0)
-    step = 2
+    step = 4
 
     def scatter(i, carry):
         for j in range(step):
             a = i * step + j
             row = state[pl.ds(a, 1), :]
-            for k in range(0, corners, ACCS):
-                at = [pl.ds(index[(k + m) * cells + a], 1) for m in range(ACCS)]
-                new = [accs[m][at[m], :] + row * weight[(k + m) * cells + a] for m in range(ACCS)]
-                for m in range(ACCS):
-                    accs[m][at[m], :] = new[m]
+            codes = [word[k][a] for k in range(corners)]
+            at = [pl.ds(code & ROW_MASK, 1) for code in codes]
+            new = [accs[k][at[k], :] + row * jnp.full((1, bins), codes[k], I32).astype(F32) for k in range(corners)]
+            for k in range(corners):
+                accs[k][at[k], :] = new[k]
         return carry
 
     lax.fori_loop(0, cells // step, scatter, 0)
 
     def merge(i, carry):
         here = pl.ds(pl.multiple_of(i * chunk, chunk), chunk)
-        total = out[here, :]
-        for acc in more:
+        total = accs[0][here, :]
+        for acc in accs[1:]:
             total = total + acc[here, :]
-        out[here, :] = total
-        return carry
-
-    lax.fori_loop(0, out.shape[0] // chunk, merge, 0)
-
-
-def return_kernel(n_lat, n_lon, cells, cap, slots, sums, out, back, send_sem, recv_sem):
+        table[here, :] = total
+        pltpu.make_async_copy(table.at[here], sums.at[here], out_sem).start()
+        return carry
+
+    lax.fori_loop(0, entries // chunk, merge, 0)
+    pltpu.make_async_copy(table, sums, out_sem).wait()
+
+
+def return_kernel(n_lat, n_lon, cells, cap, slots, sums, out, back, own_sem, send_sem, recv_sem):
     place = Place(n_lat, n_lon)
     place.greet()
 
     def copy(u, v):
         b = 3 * u + v
         return pltpu.make_async_remote_copy(
-            src_ref=sums.at[pl.ds(cells + b * cap, cap)], dst_ref=back.at[b], send_sem=send_sem.at[b],
+            src_ref=sums.at[pl.ds(cells + slot(u, v) * cap, cap)], dst_ref=back.at[b], send_sem=send_sem.at[b],
             recv_sem=recv_sem.at[b], device_id=place.at(u, v), device_id_type=MESH)
 
     for u, v in ORDER:
         @pl.when(place.has(u))
         def _():
             copy(u, v).start()
-    out[...] = sums[pl.ds(0, cells), :]
+    keep = pltpu.make_async_copy(sums.at[pl.ds(0, cells)], out, own_sem)
+    keep.start()
+    keep.wait()
     tile = 256
     bins = out.shape[1]
     number = lax.broadcasted_iota(I32, (tile, cap), 0).astype(I16)
@@ -225,7 +249,7 @@
     cells = levels * lat_cells * lon_cells
     blocks, cap = send_list.shape[2:]
     corners = departure.shape[0]
-    entries = cells + blocks * cap
+    entries = cells + (blocks - 1) * cap
     own = concentration.reshape(cells, bins)
     dma = pltpu.SemaphoreType.DMA
     table = pl.pallas_call(
@@ -234,26 +258,31 @@
         in_specs=[SMEM, VMEM], out_specs=ANY,
         scratch_shapes=[pltpu.VMEM((blocks, cap, bins), F32), dma, dma((blocks,)), dma((blocks,))],
         compiler_params=pltpu.CompilerParams(
-            collective_id=0, has_side_effects=True, vmem_limit_bytes=16 * 2**20),
+            collective_id=0, has_side_effects=True, vmem_limit_bytes=56 * 2**20),
     )(send_list.reshape(blocks * cap), own)
     forward, inverse = spectral_tables(bins)
     fwd_hi, fwd_lo = split(jnp.asarray(forward))
     inv_hi, inv_lo = split(jnp.asarray(inverse))
+    row = jnp.where(departure < cells + 5 * cap, departure, departure - cap)
+    high = jnp.round((weights * 2.0**31 - row.astype(F32)) * 2.0**-ROW_BITS)
+    high = jnp.clip(high, 0.0, 2.0 ** (31 - ROW_BITS) - 1.0).astype(I32)
+    words = (high * 2**ROW_BITS + row).reshape(-1)
     sums = pl.pallas_call(
         functools.partial(cell_kernel, cells, corners),
         out_shape=jax.ShapeDtypeStruct((entries, bins), F32),
-        in_specs=[SMEM, SMEM] + [VMEM] * 7, out_specs=VMEM,
-        scratch_shapes=[pltpu.VMEM((cells, bins), F32)] + [pltpu.VMEM((entries, bins), F32)] * (ACCS - 1),
-        compiler_params=pltpu.CompilerParams(vmem_limit_bytes=48 * 2**20),
-    )(departure.reshape(-1), weights.reshape(-1), table, cotangent.reshape(cells, bins),
-      coag_rate.reshape(cells, 1), fwd_hi, fwd_lo, inv_hi, inv_lo)
+        in_specs=[ANY, ANY] + [VMEM] * 6, out_specs=ANY,
+        scratch_shapes=[pltpu.VMEM((entries, bins), F32), pltpu.VMEM((cells, bins), F32)]
+        + [pltpu.VMEM((entries, bins), F32)] * corners + [pltpu.SMEM((cells,), I32)] * corners
+        + [dma((corners,)), dma, dma],
+        compiler_params=pltpu.CompilerParams(vmem_limit_bytes=56 * 2**20),
+    )(words, table, cotangent.reshape(cells, bins), coag_rate.reshape(cells, 1), fwd_hi, fwd_lo, inv_hi, inv_lo)
     total = pl.pallas_call(
         functools.partial(return_kernel, n_lat, n_lon, cells, cap),
         out_shape=jax.ShapeDtypeStruct((cells, bins), F32),
-        in_specs=[VMEM, VMEM], out_specs=VMEM,
-        scratch_shapes=[pltpu.VMEM((blocks, cap, bins), F32), dma((blocks,)), dma((blocks,))],
+        in_specs=[VMEM, ANY], out_specs=VMEM,
+        scratch_shapes=[pltpu.VMEM((blocks, cap, bins), F32), dma, dma((blocks,)), dma((blocks,))],
         compiler_params=pltpu.CompilerParams(
-            collective_id=1, has_side_effects=True, vmem_limit_bytes=32 * 2**20),
+            collective_id=1, has_side_effects=True, vmem_limit_bytes=56 * 2**20),
     )(send_list.reshape(blocks, cap), sums)
     return total.reshape(levels, lat_cells, lon_cells, bins)
 

time: 164 us -> 151 us (0.921)
  Pallas kernels: 152 us -> 143 us
  local copies, waits for them, and re-layouts: 9.06 us -> 5.28 us
    pallas_call x1, Pallas kernels: 59.3 us -> 47.5 us  [on_device(): pl.pallas_call(functools.partial(cell_kernel, cells, corners), out_shape=...]
    unnamed x28 -> x10, local copies, waits for them, and re-layouts: 8.11 us -> 2.92 us
    pallas_call x1, Pallas kernels: 45.5 us -> 47.5 us  [on_device(): pl.pallas_call(functools.partial(return_kernel, n_lat, n_lon, cells, cap)...]
where the time goes in v2:
time: 151 us; the launch traced here: 148 us
  Pallas kernels  143 us (95%)
  local copies, waits for them, and re-layouts  5.28 us (3%)
    pallas_call x1, Pallas kernels, on_device(): pl.pallas_call(functools.partial(send_kernel, n_lat, n_lon, cells, cap),...  47.8 us
    pallas_call x1, Pallas kernels, on_device(): pl.pallas_call(functools.partial(return_kernel, n_lat, n_lon, cells, cap)...  47.5 us
    pallas_call x1, Pallas kernels, on_device(): pl.pallas_call(functools.partial(cell_kernel, cells, corners), out_shape=...  47.5 us

profile of v2, /device:TPU:17, one launch (start us, length us, event | category | flops | bytes accessed | tf_op | source)
XLA Modules:
  0.0 148.4 jit_solution(2879933761246572706)
XLA Ops:
  0.0 0.0 copy-start.3
  0.0 0.0 copy-start.1
  0.0 0.0 copy-start
  0.0 47.8 %shard_map.82.refs_1_ = f32[10240,128]{1,0:T(8,128)} custom-call(s32[9216]{0:T(1024)} %bitcast.13, f32[2048,128]{1,0:T(8,128)} %bitcast.11), custom_call_target="tpu_custom_call" | custom-call | tf_op jit(solution)/shard_map/pallas_call | solution.py:255
  47.8 0.0 copy-done.3
  47.8 1.6 %reshape.28.refs_3_ = f32[2048,1]{1,0:T(8,128)} reshape(f32[8,16,16]{2,1,0:T(8,128)S(1)} %copy-done.3) | data formatting | bytes 16384 | tf_op jit(solution)/shard_map/reshape | solution.py:278
  49.4 0.0 copy-done.1
  49.4 0.0 copy-done
  49.4 0.2 multiply_add_fusion
  49.6 0.8 reshape.22.refs_0_
  50.4 0.0 copy-start.2
  50.4 47.5 %shard_map.83.sums = f32[10240,128]{1,0:T(8,128)} custom-call(s32[16384]{0:T(1024)} %reshape.22.refs_0_, f32[10240,128]{1,0:T(8,128)} %shard_map.82.refs_1_, f32[2048,128]{1,0:T(8,128)} %bitcast.10, f32[2048,1]{1,0:T(8,128)} %reshape.28.refs_3_, bf16[128,256]{1,0:T(8,128)(2,1)} %constant.22.refs_4_, bf16[128,256]{1,0:T(8,128)(2,1)} %constant.25.refs_5_, ...), custom_call_target="tpu_custom_call" | custom-call | tf_op jit(solution)/shard_map/pallas_call | solution.py:270
  97.9 0.0 copy-done.2
  97.9 0.6 copy.12
  98.5 47.5 %shard_map.84 = f32[2048,128]{1,0:T(8,128)} custom-call(s32[9,1024]{1,0:T(8,128)} %bitcast.12, f32[10240,128]{1,0:T(8,128)} %shard_map.83.sums), custom_call_target="tpu_custom_call" | custom-call | tf_op jit(solution)/shard_map/pallas_call | solution.py:279
  146.1 2.3 %copy.14 = f32[8,16,16,128]{3,2,1,0:T(8,128)} copy(f32[8,16,16,128]{3,2,1,0:T(8,128)} %bitcast.9) | data formatting | bytes 2097152
Async XLA Ops:
  0.0 47.8 %copy-start.3 = (f32[8,16,16]{2,1,0:T(8,128)S(1)}, f32[8,16,16]{2,1,0:T(8,128)}, u32[]{:S(2)}) copy-start(f32[8,16,16]{2,1,0:T(8,128)} %param.10) | copy-start | bytes 24580
  0.0 49.4 %copy-start.1 = (f32[8,8,16,16]{3,2,1,0:T(8,128)S(1)}, f32[8,8,16,16]{3,2,1,0:T(8,128)}, u32[]{:S(2)}) copy-start(f32[8,8,16,16]{3,2,1,0:T(8,128)} %param.11) | copy-start | bytes 196612
  0.0 49.4 %copy-start = (s32[8,8,16,16]{3,2,1,0:T(8,128)S(1)}, s32[8,8,16,16]{3,2,1,0:T(8,128)}, u32[]{:S(2)}) copy-start(s32[8,8,16,16]{3,2,1,0:T(8,128)} %param.12) | copy-start | bytes 196612
  50.4 47.5 %copy-start.2 = (s32[1,1,9,1024]{3,1,2,0:T(1,128)S(1)}, s32[1,1,9,1024]{3,1,2,0:T(1,128)}, u32[]{:S(2)}) copy-start(s32[1,1,9,1024]{3,1,2,0:T(1,128)} %param.13) | copy-start | bytes 110596

commit v3 on v2

--- a/solution.py
+++ b/solution.py
@@ -17,9 +17,6 @@
 VMEM = pl.BlockSpec(memory_space=pltpu.VMEM)
 ANY = pl.BlockSpec(memory_space=pl.ANY)
 ORDER = ((0, 0), (2, 2), (0, 2), (2, 0), (1, 0), (1, 2), (0, 1), (2, 1))
-ROW_BITS = 14
-ROW_MASK = 2**ROW_BITS - 1
-WORD_UNIT = 2.0**-31
 
 
 def split(x):
@@ -74,7 +71,8 @@
         pl.semaphore_wait(barrier, count)
 
 
-def send_kernel(n_lat, n_lon, cells, cap, slots, own, table, rows, own_sem, send_sem, recv_sem):
+def send_kernel(n_lat, n_lon, cells, cap, slots, own, weights, table, spread, rows, wide, own_sem, wide_sem, send_sem,
+                recv_sem):
     place = Place(n_lat, n_lon)
     place.greet()
     keep = pltpu.make_async_copy(own, table.at[pl.ds(0, cells)], own_sem)
@@ -100,7 +98,25 @@
 
             lax.fori_loop(0, cap // step, gather, 0)
             copy(u, v).start()
+    corners, levels, high, long = weights.shape
+    bins = own.shape[1]
+    per_level = high * long * corners
+
+    def widen(level, carry):
+        values = weights[:, level]
+        start = level * per_level
+        for i in range(high):
+            line = values[:, i, :]
+            for j in range(long):
+                at = pl.multiple_of(start + (i * long + j) * corners, corners)
+                wide[pl.ds(at, corners), :] = jnp.broadcast_to(line[:, j:j + 1], (corners, bins))
+        return carry
+
+    lax.fori_loop(0, levels, widen, 0)
+    store = pltpu.make_async_copy(wide, spread, wide_sem)
+    store.start()
     keep.wait()
+    store.wait()
     for u, v in ORDER:
         @pl.when(place.has(u))
         def _():
@@ -112,43 +128,47 @@
 
 
 def cell_kernel(cells, corners, *refs):
-    (words, table_hbm, cot, rate, fwd_hi, fwd_lo, inv_hi, inv_lo, sums), refs = refs[:9], refs[9:]
-    table, state, refs = refs[0], refs[1], refs[2:]
+    (named, spread, table_hbm, cot, rate, fwd_hi, fwd_lo, inv_hi, inv_lo, sums), refs = refs[:10], refs[10:]
+    (table, state, wide), refs = refs[:3], refs[3:]
     accs, refs = refs[:corners], refs[corners:]
-    word, (word_sem, table_sem, out_sem) = refs[:corners], refs[corners:]
+    index, (index_sem, table_sem, wide_sem, out_sem) = refs[:corners], refs[corners:]
     entries, bins = table.shape
     load = pltpu.make_async_copy(table_hbm, table, table_sem)
     load.start()
-    loads = [pltpu.make_async_copy(words.at[pl.ds(k * cells, cells)], word[k], word_sem.at[k]) for k in range(corners)]
+    loads = [pltpu.make_async_copy(named.at[pl.ds(k * cells, cells)], index[k], index_sem.at[k]) for k in range(corners)]
     for copy in loads:
         copy.start()
-    chunk = 512
-
-    def clear(i, carry):
-        for acc in accs:
-            acc[pl.ds(pl.multiple_of(i * chunk, chunk), chunk), :] = jnp.zeros((chunk, bins), F32)
-        return carry
-
-    lax.fori_loop(0, entries // chunk, clear, 0)
+    parts = 4
+    part = cells // parts
+    wides = []
+    for p in range(parts):
+        here = pl.ds(p * part * corners, part * corners)
+        wides.append(pltpu.make_async_copy(spread.at[here], wide.at[here], wide_sem.at[p]))
+        wides[p].start()
     for copy in loads:
         copy.wait()
     load.wait()
-    step = 4
+    step = 16
+    clear = entries * step // cells
 
     def gather(i, carry):
         for j in range(step):
             a = i * step + j
             total = None
             for k in range(corners):
-                code = word[k][a]
-                row = table[pl.ds(code & ROW_MASK, 1), :] * jnp.full((1, bins), code, I32).astype(F32)
+                row = table[pl.ds(index[k][a], 1), :] * wide[pl.ds(a * corners + k, 1), :]
                 total = row if total is None else total + row
             state[pl.ds(a, 1), :] = total
-        return carry
-
-    lax.fori_loop(0, cells // step, gather, 0)
+        for acc in accs:
+            acc[pl.ds(pl.multiple_of(i * clear, clear), clear), :] = jnp.zeros((clear, bins), F32)
+        return carry
+
+    for p in range(parts):
+        wides[p].wait()
+        lax.fori_loop(p * part // step, (p + 1) * part // step, gather, 0)
     tile = 256
     first = lax.broadcasted_iota(I32, (tile, bins), 1) == 0
+    diagonal = lax.broadcasted_iota(I32, (bins, bins), 0) == lax.broadcasted_iota(I32, (bins, bins), 1)
 
     def dot3(x, hi, lo):
         xh, xl = split(x)
@@ -158,7 +178,7 @@
 
     def react(i, carry):
         here = pl.ds(pl.multiple_of(i * tile, tile), tile)
-        t = state[here, :] * WORD_UNIT
+        t = state[here, :]
         c = cot[here, :]
         ts = dot3(t, fwd_hi, fwd_lo)
         cs = dot3(c, fwd_hi, fwd_lo)
@@ -169,24 +189,25 @@
         lagged = dot3(jnp.concatenate([real, imag], axis=1), inv_hi, inv_lo)
         totals = jnp.sum(t, axis=1, keepdims=True)
         weighed = jnp.sum(t * c, axis=1, keepdims=True)
-        state[here, :] = (c + rate[here, :] * (lagged - totals * c - weighed)) * WORD_UNIT
+        speed = [jnp.sum(jnp.where(diagonal, rate[pl.ds(i * (tile // bins) + h, 1), :], 0.0), axis=1, keepdims=True)
+                 for h in range(tile // bins)]
+        state[here, :] = c + jnp.concatenate(speed, axis=0) * (lagged - totals * c - weighed)
         return carry
 
     lax.fori_loop(0, cells // tile, react, 0)
-    step = 4
 
     def scatter(i, carry):
         for j in range(step):
             a = i * step + j
             row = state[pl.ds(a, 1), :]
-            codes = [word[k][a] for k in range(corners)]
-            at = [pl.ds(code & ROW_MASK, 1) for code in codes]
-            new = [accs[k][at[k], :] + row * jnp.full((1, bins), codes[k], I32).astype(F32) for k in range(corners)]
+            at = [pl.ds(index[k][a], 1) for k in range(corners)]
+            new = [accs[k][at[k], :] + row * wide[pl.ds(a * corners + k, 1), :] for k in range(corners)]
             for k in range(corners):
                 accs[k][at[k], :] = new[k]
         return carry
 
     lax.fori_loop(0, cells // step, scatter, 0)
+    chunk = 512
 
     def merge(i, carry):
         here = pl.ds(pl.multiple_of(i * chunk, chunk), chunk)
@@ -201,7 +222,7 @@
     pltpu.make_async_copy(table, sums, out_sem).wait()
 
 
-def return_kernel(n_lat, n_lon, cells, cap, slots, sums, out, back, own_sem, send_sem, recv_sem):
+def return_kernel(n_lat, n_lon, cells, cap, slots, sums, out, back, send_sem, recv_sem):
     place = Place(n_lat, n_lon)
     place.greet()
 
@@ -215,24 +236,24 @@
         @pl.when(place.has(u))
         def _():
             copy(u, v).start()
-    keep = pltpu.make_async_copy(sums.at[pl.ds(0, cells)], out, own_sem)
-    keep.start()
-    keep.wait()
+    out[...] = jnp.zeros_like(out)
     tile = 256
     bins = out.shape[1]
-    number = lax.broadcasted_iota(I32, (tile, cap), 0).astype(I16)
+    number = lax.broadcasted_iota(I32, (tile, bins), 0).astype(I16)
     for u, v in ORDER[6:] + ORDER[:6]:
         @pl.when(place.has(2 - u))
         def _():
             b = 3 * u + v
             copy(u, v).wait_recv()
             rows = jnp.concatenate(split(back[b]), axis=1)
-            named = slots[pl.ds(b, 1), :]
+            lines = cap // bins
+            named = [slots[pl.ds(b * lines + q, 1), :] for q in range(lines)]
 
             def add(i, carry):
                 here = pl.ds(pl.multiple_of(i * tile, tile), tile)
-                hit = (named - i * tile).astype(I16) == number
-                pick = jnp.where(hit, jnp.ones((), BF16), jnp.zeros((), BF16))
+                hits = [(line - i * tile).astype(I16) == number for line in named]
+                pick = jnp.concatenate(
+                    [jnp.where(hit, jnp.ones((), BF16), jnp.zeros((), BF16)) for hit in hits], axis=1)
                 got = jnp.dot(pick, rows, preferred_element_type=F32)
                 out[here, :] += got[:, :bins] + got[:, bins:]
                 return carry
@@ -252,38 +273,39 @@
     entries = cells + (blocks - 1) * cap
     own = concentration.reshape(cells, bins)
     dma = pltpu.SemaphoreType.DMA
-    table = pl.pallas_call(
+    table, spread = pl.pallas_call(
         functools.partial(send_kernel, n_lat, n_lon, cells, cap),
-        out_shape=jax.ShapeDtypeStruct((entries, bins), F32),
-        in_specs=[SMEM, VMEM], out_specs=ANY,
-        scratch_shapes=[pltpu.VMEM((blocks, cap, bins), F32), dma, dma((blocks,)), dma((blocks,))],
+        out_shape=[jax.ShapeDtypeStruct((entries, bins), F32), jax.ShapeDtypeStruct((cells * corners, bins), F32)],
+        in_specs=[SMEM, VMEM, VMEM], out_specs=[ANY, ANY],
+        scratch_shapes=[pltpu.VMEM((blocks, cap, bins), F32), pltpu.VMEM((cells * corners, bins), F32), dma, dma,
+                        dma((blocks,)), dma((blocks,))],
         compiler_params=pltpu.CompilerParams(
             collective_id=0, has_side_effects=True, vmem_limit_bytes=56 * 2**20),
-    )(send_list.reshape(blocks * cap), own)
+    )(send_list.reshape(blocks * cap), own, weights)
     forward, inverse = spectral_tables(bins)
     fwd_hi, fwd_lo = split(jnp.asarray(forward))
     inv_hi, inv_lo = split(jnp.asarray(inverse))
-    row = jnp.where(departure < cells + 5 * cap, departure, departure - cap)
-    high = jnp.round((weights * 2.0**31 - row.astype(F32)) * 2.0**-ROW_BITS)
-    high = jnp.clip(high, 0.0, 2.0 ** (31 - ROW_BITS) - 1.0).astype(I32)
-    words = (high * 2**ROW_BITS + row).reshape(-1)
+    named = jnp.where(departure < cells + 5 * cap, departure, departure - cap).reshape(-1)
     sums = pl.pallas_call(
         functools.partial(cell_kernel, cells, corners),
         out_shape=jax.ShapeDtypeStruct((entries, bins), F32),
-        in_specs=[ANY, ANY] + [VMEM] * 6, out_specs=ANY,
-        scratch_shapes=[pltpu.VMEM((entries, bins), F32), pltpu.VMEM((cells, bins), F32)]
+        in_specs=[ANY, ANY, ANY] + [VMEM] * 6, out_specs=ANY,
+        scratch_shapes=[pltpu.VMEM((entries, bins), F32), pltpu.VMEM((cells, bins), F32),
+                        pltpu.VMEM((cells * corners, bins), F32)]
         + [pltpu.VMEM((entries, bins), F32)] * corners + [pltpu.SMEM((cells,), I32)] * corners
-        + [dma((corners,)), dma, dma],
-        compiler_params=pltpu.CompilerParams(vmem_limit_bytes=56 * 2**20),
-    )(words, table, cotangent.reshape(cells, bins), coag_rate.reshape(cells, 1), fwd_hi, fwd_lo, inv_hi, inv_lo)
+        + [dma((corners,)), dma, dma((4,)), dma],
+        compiler_params=pltpu.CompilerParams(vmem_limit_bytes=60 * 2**20),
+    )(named, spread, table, cotangent.reshape(cells, bins), coag_rate.reshape(cells // bins, bins), fwd_hi, fwd_lo,
+      inv_hi, inv_lo)
     total = pl.pallas_call(
         functools.partial(return_kernel, n_lat, n_lon, cells, cap),
         out_shape=jax.ShapeDtypeStruct((cells, bins), F32),
         in_specs=[VMEM, ANY], out_specs=VMEM,
-        scratch_shapes=[pltpu.VMEM((blocks, cap, bins), F32), dma, dma((blocks,)), dma((blocks,))],
+        scratch_shapes=[pltpu.VMEM((blocks, cap, bins), F32), dma((blocks,)), dma((blocks,))],
         compiler_params=pltpu.CompilerParams(
             collective_id=1, has_side_effects=True, vmem_limit_bytes=56 * 2**20),
-    )(send_list.reshape(blocks, cap), sums)
+    )(send_list.reshape(blocks * cap // bins, bins), sums)
+    total = total + sums[:cells]
     return total.reshape(levels, lat_cells, lon_cells, bins)
 
 

time: 151 us -> 141 us (0.934)
  Pallas kernels: 143 us -> 133 us
  other arithmetic: 0.19 us -> 3.71 us
  local copies, waits for them, and re-layouts: 5.28 us -> 2.33 us
    pallas_call x1, Pallas kernels: 47.5 us -> 37.5 us  [on_device(): pl.pallas_call(functools.partial(cell_kernel, cells, corners), out_shape=...]
    unnamed x10 -> x0, local copies, waits for them, and re-layouts: 2.92 us -> none
    add x1, other arithmetic: 0.19 us -> 2.62 us  [on_device(): total = total + sums[:cells]]
where the time goes in v3:
time: 141 us; the launch traced here: 139 us
  Pallas kernels  133 us (94%)
  other arithmetic  3.71 us (3%)
  local copies, waits for them, and re-layouts  2.33 us (2%)
    pallas_call x1, Pallas kernels, on_device(): pl.pallas_call(functools.partial(send_kernel, n_lat, n_lon, cells, cap),...  47.7 us
    pallas_call x1, Pallas kernels, on_device(): pl.pallas_call(functools.partial(return_kernel, n_lat, n_lon, cells, cap)...  47.4 us
    pallas_call x1, Pallas kernels, on_device(): pl.pallas_call(functools.partial(cell_kernel, cells, corners), out_shape=...  37.5 us

profile of v3, /device:TPU:17, one launch (start us, length us, event | category | flops | bytes accessed | tf_op | source)
XLA Modules:
  0.0 138.8 jit_solution(11276538239812094136)
XLA Ops:
  0.0 1.5 %reshape.26.refs_4_ = f32[16,128]{1,0:T(8,128)} reshape(f32[8,16,16]{2,1,0:T(8,128)} %param.10) | data formatting | bytes 16384 | tf_op jit(solution)/shard_map/reshape | solution.py:298
  1.5 1.1 compare_select_fusion
  2.6 0.8 reshape.22.refs_0_
  3.4 47.7 %shard_map.82 = (f32[10240,128]{1,0:T(8,128)}, f32[16384,128]{1,0:T(8,128)}) custom-call(s32[9216]{0:T(1024)} %bitcast.9, f32[2048,128]{1,0:T(8,128)} %bitcast.8, f32[8,8,16,16]{3,2,1,0:T(8,128)} %weights.1), custom_call_target="tpu_custom_call" | custom-call | tf_op jit(solution)/shard_map/pallas_call | solution.py:276
  51.2 37.5 %shard_map.83.sums = f32[10240,128]{1,0:T(8,128)} custom-call(s32[16384]{0:T(1024)} %reshape.22.refs_0_, f32[16384,128]{1,0:T(8,128)} %get-tuple-element.7.refs_1_, f32[10240,128]{1,0:T(8,128)} %get-tuple-element.8.refs_2_, f32[2048,128]{1,0:T(8,128)} %bitcast.7, f32[16,128]{1,0:T(8,128)} %reshape.26.refs_4_, bf16[128,256]{1,0:T(8,128)(2,1)} %constant.12.refs_5_, ...), custom_call_target="tpu_custom_call" | custom-call | tf_op jit(solution)/shard_map/pallas_call | solution.py:289
  88.7 47.4 %shard_map.84 = f32[2048,128]{1,0:T(8,128)} custom-call(s32[72,128]{1,0:T(8,128)} %bitcast.10, f32[10240,128]{1,0:T(8,128)} %shard_map.83.sums), custom_call_target="tpu_custom_call" | custom-call | tf_op jit(solution)/shard_map/pallas_call | solution.py:300
  136.2 2.6 %slice_add_fusion = f32[2048,128]{1,0:T(8,128)} fusion(f32[2048,128]{1,0:T(8,128)} %shard_map.84, f32[10240,128]{1,0:T(8,128)} %shard_map.83.sums), kind=kLoop, calls=%fused_computation.1 | loop fusion | flops 262144 | bytes 3145728 | tf_op jit(solution)/shard_map/add | solution.py:308

commit v4 on v3

--- a/solution.py
+++ b/solution.py
@@ -71,8 +71,8 @@
         pl.semaphore_wait(barrier, count)
 
 
-def send_kernel(n_lat, n_lon, cells, cap, slots, own, weights, table, spread, rows, wide, own_sem, wide_sem, send_sem,
-                recv_sem):
+def send_kernel(n_lat, n_lon, cells, cap, slots, own, weights, departure, table, spread, named, rows, wide, flat, own_sem,
+                wide_sem, flat_sem, send_sem, recv_sem):
     place = Place(n_lat, n_lon)
     place.greet()
     keep = pltpu.make_async_copy(own, table.at[pl.ds(0, cells)], own_sem)
@@ -115,8 +115,26 @@
     lax.fori_loop(0, levels, widen, 0)
     store = pltpu.make_async_copy(wide, spread, wide_sem)
     store.start()
+    packs = bins // long
+    mine = lax.broadcasted_iota(I32, (high, bins), 1) // long == lax.broadcasted_iota(I32, (high, bins), 0) % packs
+
+    def flatten(k, carry):
+        lines = []
+        for level in range(levels):
+            value = departure[k, level]
+            value = jnp.where(value < cells + 5 * cap, value, value - cap)
+            value = jnp.where(mine, jnp.concatenate([value] * packs, axis=1), 0)
+            lines += [jnp.sum(value[h:h + packs], axis=0, keepdims=True) for h in range(0, high, packs)]
+        count = len(lines)
+        flat[pl.ds(pl.multiple_of(k * count, count), count), :] = jnp.concatenate(lines, axis=0)
+        return carry
+
+    lax.fori_loop(0, corners, flatten, 0)
+    note = pltpu.make_async_copy(flat, named, flat_sem)
+    note.start()
     keep.wait()
     store.wait()
+    note.wait()
     for u, v in ORDER:
         @pl.when(place.has(u))
         def _():
@@ -166,9 +184,10 @@
     for p in range(parts):
         wides[p].wait()
         lax.fori_loop(p * part // step, (p + 1) * part // step, gather, 0)
-    tile = 256
+    levels, high, long = rate.shape
+    tile = high * long
     first = lax.broadcasted_iota(I32, (tile, bins), 1) == 0
-    diagonal = lax.broadcasted_iota(I32, (bins, bins), 0) == lax.broadcasted_iota(I32, (bins, bins), 1)
+    diagonal = lax.broadcasted_iota(I32, (tile, long), 0) % long == lax.broadcasted_iota(I32, (tile, long), 1)
 
     def dot3(x, hi, lo):
         xh, xl = split(x)
@@ -189,9 +208,10 @@
         lagged = dot3(jnp.concatenate([real, imag], axis=1), inv_hi, inv_lo)
         totals = jnp.sum(t, axis=1, keepdims=True)
         weighed = jnp.sum(t * c, axis=1, keepdims=True)
-        speed = [jnp.sum(jnp.where(diagonal, rate[pl.ds(i * (tile // bins) + h, 1), :], 0.0), axis=1, keepdims=True)
-                 for h in range(tile // bins)]
-        state[here, :] = c + jnp.concatenate(speed, axis=0) * (lagged - totals * c - weighed)
+        lines = rate[i]
+        spread_lines = jnp.concatenate([jnp.broadcast_to(lines[h:h + 1, :], (long, long)) for h in range(high)], axis=0)
+        speed = jnp.sum(jnp.where(diagonal, spread_lines, 0.0), axis=1, keepdims=True)
+        state[here, :] = c + speed * (lagged - totals * c - weighed)
         return carry
 
     lax.fori_loop(0, cells // tile, react, 0)
@@ -232,37 +252,51 @@
             src_ref=sums.at[pl.ds(cells + slot(u, v) * cap, cap)], dst_ref=back.at[b], send_sem=send_sem.at[b],
             recv_sem=recv_sem.at[b], device_id=place.at(u, v), device_id_type=MESH)
 
-    for u, v in ORDER:
-        @pl.when(place.has(u))
-        def _():
-            copy(u, v).start()
-    out[...] = jnp.zeros_like(out)
+    def send(pairs):
+        for u, v in pairs:
+            @pl.when(place.has(u))
+            def _():
+                copy(u, v).start()
+
+    def sent(pairs):
+        for u, v in pairs:
+            @pl.when(place.has(u))
+            def _():
+                copy(u, v).wait_send()
+
     tile = 256
     bins = out.shape[1]
     number = lax.broadcasted_iota(I32, (tile, bins), 0).astype(I16)
-    for u, v in ORDER[6:] + ORDER[:6]:
-        @pl.when(place.has(2 - u))
-        def _():
-            b = 3 * u + v
-            copy(u, v).wait_recv()
-            rows = jnp.concatenate(split(back[b]), axis=1)
-            lines = cap // bins
-            named = [slots[pl.ds(b * lines + q, 1), :] for q in range(lines)]
-
-            def add(i, carry):
-                here = pl.ds(pl.multiple_of(i * tile, tile), tile)
-                hits = [(line - i * tile).astype(I16) == number for line in named]
-                pick = jnp.concatenate(
-                    [jnp.where(hit, jnp.ones((), BF16), jnp.zeros((), BF16)) for hit in hits], axis=1)
-                got = jnp.dot(pick, rows, preferred_element_type=F32)
-                out[here, :] += got[:, :bins] + got[:, bins:]
-                return carry
-
-            lax.fori_loop(0, cells // tile, add, 0)
-    for u, v in ORDER:
-        @pl.when(place.has(u))
-        def _():
-            copy(u, v).wait_send()
+
+    def collect(pairs):
+        for u, v in pairs:
+            @pl.when(place.has(2 - u))
+            def _():
+                b = 3 * u + v
+                copy(u, v).wait_recv()
+                rows = jnp.concatenate(split(back[b]), axis=1)
+                lines = cap // bins
+                named = [slots[pl.ds(b * lines + q, 1), :] for q in range(lines)]
+
+                def add(i, carry):
+                    here = pl.ds(pl.multiple_of(i * tile, tile), tile)
+                    hits = [(line - i * tile).astype(I16) == number for line in named]
+                    pick = jnp.concatenate(
+                        [jnp.where(hit, jnp.ones((), BF16), jnp.zeros((), BF16)) for hit in hits], axis=1)
+                    got = jnp.dot(pick, rows, preferred_element_type=F32)
+                    out[here, :] += got[:, :bins] + got[:, bins:]
+                    return carry
+
+                lax.fori_loop(0, cells // tile, add, 0)
+
+    send(ORDER[:4])
+    send(ORDER[6:])
+    out[...] = jnp.zeros_like(out)
+    collect(ORDER[6:])
+    sent(ORDER[:2])
+    send(ORDER[4:6])
+    collect(ORDER[:6])
+    sent(ORDER[2:])
 
 
 def on_device(n_lat, n_lon, concentration, cotangent, coag_rate, weights, departure, send_list):
@@ -273,19 +307,19 @@
     entries = cells + (blocks - 1) * cap
     own = concentration.reshape(cells, bins)
     dma = pltpu.SemaphoreType.DMA
-    table, spread = pl.pallas_call(
+    table, spread, named = pl.pallas_call(
         functools.partial(send_kernel, n_lat, n_lon, cells, cap),
-        out_shape=[jax.ShapeDtypeStruct((entries, bins), F32), jax.ShapeDtypeStruct((cells * corners, bins), F32)],
-        in_specs=[SMEM, VMEM, VMEM], out_specs=[ANY, ANY],
-        scratch_shapes=[pltpu.VMEM((blocks, cap, bins), F32), pltpu.VMEM((cells * corners, bins), F32), dma, dma,
-                        dma((blocks,)), dma((blocks,))],
+        out_shape=[jax.ShapeDtypeStruct((entries, bins), F32), jax.ShapeDtypeStruct((cells * corners, bins), F32),
+                   jax.ShapeDtypeStruct((corners * cells // bins, bins), I32)],
+        in_specs=[SMEM, VMEM, VMEM, VMEM], out_specs=[ANY, ANY, ANY],
+        scratch_shapes=[pltpu.VMEM((blocks, cap, bins), F32), pltpu.VMEM((cells * corners, bins), F32),
+                        pltpu.VMEM((corners * cells // bins, bins), I32), dma, dma, dma, dma((blocks,)), dma((blocks,))],
         compiler_params=pltpu.CompilerParams(
             collective_id=0, has_side_effects=True, vmem_limit_bytes=56 * 2**20),
-    )(send_list.reshape(blocks * cap), own, weights)
+    )(send_list.reshape(blocks * cap), own, weights, departure)
     forward, inverse = spectral_tables(bins)
     fwd_hi, fwd_lo = split(jnp.asarray(forward))
     inv_hi, inv_lo = split(jnp.asarray(inverse))
-    named = jnp.where(departure < cells + 5 * cap, departure, departure - cap).reshape(-1)
     sums = pl.pallas_call(
         functools.partial(cell_kernel, cells, corners),
         out_shape=jax.ShapeDtypeStruct((entries, bins), F32),
@@ -295,7 +329,7 @@
         + [pltpu.VMEM((entries, bins), F32)] * corners + [pltpu.SMEM((cells,), I32)] * corners
         + [dma((corners,)), dma, dma((4,)), dma],
         compiler_params=pltpu.CompilerParams(vmem_limit_bytes=60 * 2**20),
-    )(named, spread, table, cotangent.reshape(cells, bins), coag_rate.reshape(cells // bins, bins), fwd_hi, fwd_lo,
+    )(named.reshape(-1), spread, table, cotangent.reshape(cells, bins), coag_rate, fwd_hi, fwd_lo,
       inv_hi, inv_lo)
     total = pl.pallas_call(
         functools.partial(return_kernel, n_lat, n_lon, cells, cap),

time: 141 us -> 136 us (0.965)
  local copies, waits for them, and re-layouts: 2.33 us -> 0 us
    reshape x2 -> x0, local copies, waits for them, and re-layouts: 2.33 us -> none  [the longest x1 1.52 us: on_device(): coag_rate.reshape(cells // bins, bins)]
where the time goes in v4:
time: 136 us; the launch traced here: 135 us
  Pallas kernels  132 us (97%)
  other arithmetic  2.62 us (2%)
    pallas_call x1, Pallas kernels, on_device(): pl.pallas_call(functools.partial(send_kernel, n_lat, n_lon, cells, cap),...  47.9 us
    pallas_call x1, Pallas kernels, on_device(): pl.pallas_call(functools.partial(return_kernel, n_lat, n_lon, cells, cap)...  46.8 us
    pallas_call x1, Pallas kernels, on_device(): pl.pallas_call(functools.partial(cell_kernel, cells, corners), out_shape=...  37.5 us

profile of v4, /device:TPU:17, one launch (start us, length us, event | category | flops | bytes accessed | tf_op | source)
XLA Modules:
  0.0 134.8 jit_solution(8493929321363065863)
XLA Ops:
  0.0 47.9 %shard_map.82 = (f32[10240,128]{1,0:T(8,128)}, f32[16384,128]{1,0:T(8,128)}, s32[128,128]{1,0:T(8,128)}) custom-call(s32[9216]{0:T(1024)} %bitcast.8, f32[2048,128]{1,0:T(8,128)} %bitcast.7, f32[8,8,16,16]{3,2,1,0:T(8,128)} %weights.1, s32[8,8,16,16]{3,2,1,0:T(8,128)} %departure.1), custom_call_target="tpu_custom_call" | custom-call | tf_op jit(solution)/shard_map/pallas_call | solution.py:310
  47.9 37.5 %shard_map.83.sums = f32[10240,128]{1,0:T(8,128)} custom-call(s32[16384]{0:T(1024)} %bitcast.10, f32[16384,128]{1,0:T(8,128)} %get-tuple-element.9.refs_1_, f32[10240,128]{1,0:T(8,128)} %get-tuple-element.10.refs_2_, f32[2048,128]{1,0:T(8,128)} %bitcast.6, f32[8,16,16]{2,1,0:T(8,128)} %refs_4_.1, bf16[128,256]{1,0:T(8,128)(2,1)} %constant.7.refs_5_, ...), custom_call_target="tpu_custom_call" | custom-call | tf_op jit(solution)/shard_map/pallas_call | solution.py:323
  85.4 46.8 %shard_map.84 = f32[2048,128]{1,0:T(8,128)} custom-call(s32[72,128]{1,0:T(8,128)} %bitcast.9, f32[10240,128]{1,0:T(8,128)} %shard_map.83.sums), custom_call_target="tpu_custom_call" | custom-call | tf_op jit(solution)/shard_map/pallas_call | solution.py:334
  132.2 2.6 %slice_add_fusion = f32[2048,128]{1,0:T(8,128)} fusion(f32[2048,128]{1,0:T(8,128)} %shard_map.84, f32[10240,128]{1,0:T(8,128)} %shard_map.83.sums), kind=kLoop, calls=%fused_computation | loop fusion | flops 262144 | bytes 3145728 | tf_op jit(solution)/shard_map/add | solution.py:342

commit v5 on v4

--- a/solution.py
+++ b/solution.py
@@ -16,7 +16,13 @@
 SMEM = pl.BlockSpec(memory_space=pltpu.SMEM)
 VMEM = pl.BlockSpec(memory_space=pltpu.VMEM)
 ANY = pl.BlockSpec(memory_space=pl.ANY)
-ORDER = ((0, 0), (2, 2), (0, 2), (2, 0), (1, 0), (1, 2), (0, 1), (2, 1))
+FIRST = ((1, 0), (1, 2))
+CORNER = ((0, 0), (2, 2), (0, 2), (2, 0))
+REST = ((0, 1), (2, 1))
+NEXT = CORNER + REST
+BACK = CORNER + FIRST + REST
+
+PARTS = 8
 
 
 def split(x):
@@ -63,7 +69,7 @@
 
     def greet(self):
         barrier = pltpu.get_barrier_semaphore()
-        for u, v in ORDER:
+        for u, v in FIRST + NEXT:
             @pl.when(self.has(u))
             def _():
                 pl.semaphore_signal(barrier, inc=1, device_id=self.at(u, v), device_id_type=MESH)
@@ -71,12 +77,18 @@
         pl.semaphore_wait(barrier, count)
 
 
-def send_kernel(n_lat, n_lon, cells, cap, slots, own, weights, departure, table, spread, named, rows, wide, flat, own_sem,
-                wide_sem, flat_sem, send_sem, recv_sem):
+def send_kernel(n_lat, n_lon, cells, cap, slots_in, own_in, weights_in, departure_in, table, spread, named, slots, own,
+                weights, departure, rows, wide, flat, in_sem, own_sem, wide_sem, flat_sem, send_sem, recv_sem, half_send,
+                half_recv):
+    pairs = ((slots_in, slots), (own_in, own), (weights_in, weights), (departure_in, departure))
+    loads = [pltpu.make_async_copy(source, target, in_sem.at[n]) for n, (source, target) in enumerate(pairs)]
+    for load in loads:
+        load.start()
     place = Place(n_lat, n_lon)
     place.greet()
-    keep = pltpu.make_async_copy(own, table.at[pl.ds(0, cells)], own_sem)
-    keep.start()
+    keep = pltpu.make_async_copy(own_in, table.at[pl.ds(0, cells)], own_sem)
+    loads[0].wait()
+    loads[1].wait()
 
     def copy(u, v):
         b = 3 * u + v
@@ -84,20 +96,39 @@
             src_ref=rows.at[b], dst_ref=table.at[pl.ds(cells + slot(u, v) * cap, cap)], send_sem=send_sem.at[b],
             recv_sem=recv_sem.at[b], device_id=place.at(2 - u, 2 - v), device_id_type=MESH)
 
-    for u, v in ORDER:
+    half = cap // 2
+
+    def half_copy(u, v, h):
+        b = 3 * u + v
+        sem = 2 * (v // 2) + h
+        return pltpu.make_async_remote_copy(
+            src_ref=rows.at[b, pl.ds(h * half, half)],
+            dst_ref=table.at[pl.ds(cells + slot(u, v) * cap + h * half, half)], send_sem=half_send.at[sem],
+            recv_sem=half_recv.at[sem], device_id=place.at(2 - u, 2 - v), device_id_type=MESH)
+
+    def pick(b, low, count):
+        step = 32
+
+        def gather(i, carry):
+            for j in range(step):
+                s = low + i * step + j
+                rows[b, pl.ds(s, 1), :] = own[pl.ds(slots[b * cap + s], 1), :]
+            return carry
+
+        lax.fori_loop(0, count // step, gather, 0)
+
+    for h in range(2):
+        for u, v in FIRST:
+            pick(3 * u + v, h * half, half)
+            half_copy(u, v, h).start()
+    for u, v in NEXT:
         @pl.when(place.has(2 - u))
         def _():
-            b = 3 * u + v
-            step = 32
-
-            def gather(i, carry):
-                for j in range(step):
-                    s = i * step + j
-                    rows[b, pl.ds(s, 1), :] = own[pl.ds(slots[b * cap + s], 1), :]
-                return carry
-
-            lax.fori_loop(0, cap // step, gather, 0)
+            pick(3 * u + v, 0, cap)
             copy(u, v).start()
+    keep.start()
+    loads[2].wait()
+    loads[3].wait()
     corners, levels, high, long = weights.shape
     bins = own.shape[1]
     per_level = high * long * corners
@@ -135,7 +166,11 @@
     keep.wait()
     store.wait()
     note.wait()
-    for u, v in ORDER:
+    for h in range(2):
+        for u, v in FIRST:
+            half_copy(u, v, h).wait_recv()
+            half_copy(u, v, h).wait_send()
+    for u, v in NEXT:
         @pl.when(place.has(u))
         def _():
             copy(u, v).wait_recv()
@@ -146,26 +181,34 @@
 
 
 def cell_kernel(cells, corners, *refs):
-    (named, spread, table_hbm, cot, rate, fwd_hi, fwd_lo, inv_hi, inv_lo, sums), refs = refs[:10], refs[10:]
-    (table, state, wide), refs = refs[:3], refs[3:]
+    (named, spread, table_hbm), later_in, sums, refs = refs[:3], refs[3:9], refs[9], refs[10:]
+    (table, state, wide), later, refs = refs[:3], refs[3:9], refs[9:]
+    cot, rate, fwd_hi, fwd_lo, inv_hi, inv_lo = later
     accs, refs = refs[:corners], refs[corners:]
-    index, (index_sem, table_sem, wide_sem, out_sem) = refs[:corners], refs[corners:]
+    index, (index_sem, table_sem, wide_sem, later_sem, out_sem) = refs[:corners], refs[corners:]
     entries, bins = table.shape
     load = pltpu.make_async_copy(table_hbm, table, table_sem)
     load.start()
     loads = [pltpu.make_async_copy(named.at[pl.ds(k * cells, cells)], index[k], index_sem.at[k]) for k in range(corners)]
     for copy in loads:
         copy.start()
-    parts = 4
-    part = cells // parts
-    wides = []
-    for p in range(parts):
-        here = pl.ds(p * part * corners, part * corners)
-        wides.append(pltpu.make_async_copy(spread.at[here], wide.at[here], wide_sem.at[p]))
-        wides[p].start()
+    part = cells // PARTS
+
+    def wide_copy(p):
+        here = pl.ds(pl.multiple_of(p * part * corners, part * corners), part * corners)
+        return pltpu.make_async_copy(spread.at[here], wide.at[here], wide_sem.at[p])
+
+    for p in range(2):
+        wide_copy(p).start()
     for copy in loads:
         copy.wait()
     load.wait()
+    for p in range(2, PARTS):
+        wide_copy(p).start()
+    laters = [pltpu.make_async_copy(source, target, later_sem.at[n])
+              for n, (source, target) in enumerate(zip(later_in, later))]
+    for copy in laters:
+        copy.start()
     step = 16
     clear = entries * step // cells
 
@@ -181,9 +224,14 @@
             acc[pl.ds(pl.multiple_of(i * clear, clear), clear), :] = jnp.zeros((clear, bins), F32)
         return carry
 
-    for p in range(parts):
-        wides[p].wait()
-        lax.fori_loop(p * part // step, (p + 1) * part // step, gather, 0)
+    def next_part(p, carry):
+        wide_copy(p).wait()
+        lax.fori_loop(p * (part // step), (p + 1) * (part // step), gather, 0)
+        return carry
+
+    lax.fori_loop(0, PARTS, next_part, 0)
+    for copy in laters:
+        copy.wait()
     levels, high, long = rate.shape
     tile = high * long
     first = lax.broadcasted_iota(I32, (tile, bins), 1) == 0
@@ -242,8 +290,10 @@
     pltpu.make_async_copy(table, sums, out_sem).wait()
 
 
-def return_kernel(n_lat, n_lon, cells, cap, slots, sums, out, back, send_sem, recv_sem):
+def return_kernel(n_lat, n_lon, cells, cap, slots_in, sums, out, slots, back, slots_sem, own_sem, send_sem, recv_sem):
     place = Place(n_lat, n_lon)
+    load = pltpu.make_async_copy(slots_in, slots, slots_sem)
+    load.start()
     place.greet()
 
     def copy(u, v):
@@ -289,14 +339,17 @@
 
                 lax.fori_loop(0, cells // tile, add, 0)
 
-    send(ORDER[:4])
-    send(ORDER[6:])
-    out[...] = jnp.zeros_like(out)
-    collect(ORDER[6:])
-    sent(ORDER[:2])
-    send(ORDER[4:6])
-    collect(ORDER[:6])
-    sent(ORDER[2:])
+    send(BACK[:4])
+    send(BACK[6:])
+    keep = pltpu.make_async_copy(sums.at[pl.ds(0, cells)], out, own_sem)
+    keep.start()
+    load.wait()
+    keep.wait()
+    collect(BACK[6:])
+    sent(BACK[:2])
+    send(BACK[4:6])
+    collect(BACK[:6])
+    sent(BACK[2:])
 
 
 def on_device(n_lat, n_lon, concentration, cotangent, coag_rate, weights, departure, send_list):
@@ -311,11 +364,14 @@
         functools.partial(send_kernel, n_lat, n_lon, cells, cap),
         out_shape=[jax.ShapeDtypeStruct((entries, bins), F32), jax.ShapeDtypeStruct((cells * corners, bins), F32),
                    jax.ShapeDtypeStruct((corners * cells // bins, bins), I32)],
-        in_specs=[SMEM, VMEM, VMEM, VMEM], out_specs=[ANY, ANY, ANY],
-        scratch_shapes=[pltpu.VMEM((blocks, cap, bins), F32), pltpu.VMEM((cells * corners, bins), F32),
-                        pltpu.VMEM((corners * cells // bins, bins), I32), dma, dma, dma, dma((blocks,)), dma((blocks,))],
+        in_specs=[ANY] * 4, out_specs=[ANY, ANY, ANY],
+        scratch_shapes=[pltpu.SMEM((blocks * cap,), I32), pltpu.VMEM((cells, bins), F32),
+                        pltpu.VMEM(weights.shape, F32), pltpu.VMEM(departure.shape, I32),
+                        pltpu.VMEM((blocks, cap, bins), F32), pltpu.VMEM((cells * corners, bins), F32),
+                        pltpu.VMEM((corners * cells // bins, bins), I32), dma((4,)), dma, dma, dma, dma((blocks,)), dma((blocks,)),
+                        dma((4,)), dma((4,))],
         compiler_params=pltpu.CompilerParams(
-            collective_id=0, has_side_effects=True, vmem_limit_bytes=56 * 2**20),
+            collective_id=0, has_side_effects=True, vmem_limit_bytes=60 * 2**20),
     )(send_list.reshape(blocks * cap), own, weights, departure)
     forward, inverse = spectral_tables(bins)
     fwd_hi, fwd_lo = split(jnp.asarray(forward))
@@ -323,23 +379,25 @@
     sums = pl.pallas_call(
         functools.partial(cell_kernel, cells, corners),
         out_shape=jax.ShapeDtypeStruct((entries, bins), F32),
-        in_specs=[ANY, ANY, ANY] + [VMEM] * 6, out_specs=ANY,
+        in_specs=[ANY] * 9, out_specs=ANY,
         scratch_shapes=[pltpu.VMEM((entries, bins), F32), pltpu.VMEM((cells, bins), F32),
-                        pltpu.VMEM((cells * corners, bins), F32)]
+                        pltpu.VMEM((cells * corners, bins), F32), pltpu.VMEM((cells, bins), F32),
+                        pltpu.VMEM(coag_rate.shape, F32)]
+        + [pltpu.VMEM(part.shape, BF16) for part in (fwd_hi, fwd_lo, inv_hi, inv_lo)]
         + [pltpu.VMEM((entries, bins), F32)] * corners + [pltpu.SMEM((cells,), I32)] * corners
-        + [dma((corners,)), dma, dma((4,)), dma],
+        + [dma((corners,)), dma, dma((PARTS,)), dma((6,)), dma],
         compiler_params=pltpu.CompilerParams(vmem_limit_bytes=60 * 2**20),
     )(named.reshape(-1), spread, table, cotangent.reshape(cells, bins), coag_rate, fwd_hi, fwd_lo,
       inv_hi, inv_lo)
     total = pl.pallas_call(
         functools.partial(return_kernel, n_lat, n_lon, cells, cap),
         out_shape=jax.ShapeDtypeStruct((cells, bins), F32),
-        in_specs=[VMEM, ANY], out_specs=VMEM,
-        scratch_shapes=[pltpu.VMEM((blocks, cap, bins), F32), dma((blocks,)), dma((blocks,))],
+        in_specs=[ANY, ANY], out_specs=VMEM,
+        scratch_shapes=[pltpu.VMEM((blocks * cap // bins, bins), I32), pltpu.VMEM((blocks, cap, bins), F32), dma, dma,
+                        dma((blocks,)), dma((blocks,))],
         compiler_params=pltpu.CompilerParams(
-            collective_id=1, has_side_effects=True, vmem_limit_bytes=56 * 2**20),
+            collective_id=1, has_side_effects=True, vmem_limit_bytes=60 * 2**20),
     )(send_list.reshape(blocks * cap // bins, bins), sums)
-    total = total + sums[:cells]
     return total.reshape(levels, lat_cells, lon_cells, bins)
 
 

time: 136 us -> 133 us (0.978)
  other arithmetic: 2.62 us -> 0 us
  local copies, waits for them, and re-layouts: 0 us -> 2.27 us
    add x1 -> x0, other arithmetic: 2.62 us -> none  [on_device(): total = total + sums[:cells]]
    pallas_call x1, Pallas kernels: 37.5 us -> 35.1 us  [on_device(): pl.pallas_call(functools.partial(cell_kernel, cells, corners), out_shape=...]
    unnamed x0 -> x1, local copies, waits for them, and re-layouts: none -> 2.27 us
where the time goes in v5:
time: 133 us
  Pallas kernels  131 us (98%)
  local copies, waits for them, and re-layouts  2.27 us (2%)
    pallas_call x1, Pallas kernels, on_device(): pl.pallas_call(functools.partial(send_kernel, n_lat, n_lon, cells, cap),...  48.1 us
    pallas_call x1, Pallas kernels, on_device(): pl.pallas_call(functools.partial(return_kernel, n_lat, n_lon, cells, cap)...  47.6 us
    pallas_call x1, Pallas kernels, on_device(): pl.pallas_call(functools.partial(cell_kernel, cells, corners), out_shape=...  35.1 us

profile of v5, /device:TPU:17, one launch (start us, length us, event | category | flops | bytes accessed | tf_op | source)
XLA Modules:
  0.0 133.0 jit_solution(7016746082208751147)
XLA Ops:
  0.0 48.1 %shard_map.82 = (f32[10240,128]{1,0:T(8,128)}, f32[16384,128]{1,0:T(8,128)}, s32[128,128]{1,0:T(8,128)}) custom-call(s32[9216]{0:T(1024)} %bitcast.9, f32[2048,128]{1,0:T(8,128)} %bitcast.8, f32[8,8,16,16]{3,2,1,0:T(8,128)} %weights_in.1, s32[8,8,16,16]{3,2,1,0:T(8,128)} %departure_in.1), custom_call_target="tpu_custom_call" | custom-call | tf_op jit(solution)/shard_map/pallas_call | solution.py:363
  48.1 35.1 %shard_map.83.sums = f32[10240,128]{1,0:T(8,128)} custom-call(s32[16384]{0:T(1024)} %bitcast.11, f32[16384,128]{1,0:T(8,128)} %get-tuple-element.9.refs_1_, f32[10240,128]{1,0:T(8,128)} %get-tuple-element.10.refs_2_, f32[2048,128]{1,0:T(8,128)} %bitcast.7, f32[8,16,16]{2,1,0:T(8,128)} %refs_4_.1, bf16[128,256]{1,0:T(8,128)(2,1)} %constant.7.refs_5_, ...), custom_call_target="tpu_custom_call" | custom-call | tf_op jit(solution)/shard_map/pallas_call | solution.py:379
  83.1 47.6 %shard_map.84 = f32[2048,128]{1,0:T(8,128)} custom-call(s32[72,128]{1,0:T(8,128)} %bitcast.10, f32[10240,128]{1,0:T(8,128)} %shard_map.83.sums), custom_call_target="tpu_custom_call" | custom-call | tf_op jit(solution)/shard_map/pallas_call | solution.py:392
  130.7 2.3 %copy.10 = f32[8,16,16,128]{3,2,1,0:T(8,128)} copy(f32[8,16,16,128]{3,2,1,0:T(8,128)} %bitcast.6) | data formatting | bytes 2097152

commit v6 on v5

--- a/solution.py
+++ b/solution.py
@@ -86,7 +86,7 @@
         load.start()
     place = Place(n_lat, n_lon)
     place.greet()
-    keep = pltpu.make_async_copy(own_in, table.at[pl.ds(0, cells)], own_sem)
+    keep = pltpu.make_async_copy(own, table.at[pl.ds(0, cells)], own_sem)
     loads[0].wait()
     loads[1].wait()
 
@@ -290,7 +290,8 @@
     pltpu.make_async_copy(table, sums, out_sem).wait()
 
 
-def return_kernel(n_lat, n_lon, cells, cap, slots_in, sums, out, slots, back, slots_sem, own_sem, send_sem, recv_sem):
+def return_kernel(n_lat, n_lon, cells, cap, slots_in, sums, result, slots, out, back, slots_sem, own_sem, out_sem, send_sem,
+                  recv_sem):
     place = Place(n_lat, n_lon)
     load = pltpu.make_async_copy(slots_in, slots, slots_sem)
     load.start()
@@ -335,6 +336,8 @@
                         [jnp.where(hit, jnp.ones((), BF16), jnp.zeros((), BF16)) for hit in hits], axis=1)
                     got = jnp.dot(pick, rows, preferred_element_type=F32)
                     out[here, :] += got[:, :bins] + got[:, bins:]
+                    if (u, v) == BACK[5]:
+                        pltpu.make_async_copy(out.at[here], result.at[here], out_sem).start()
                     return carry
 
                 lax.fori_loop(0, cells // tile, add, 0)
@@ -350,6 +353,21 @@
     send(BACK[4:6])
     collect(BACK[:6])
     sent(BACK[2:])
+    pltpu.make_async_copy(out, result, out_sem).wait()
+
+
+def copy_kernel(source, target, held, in_sem, out_sem):
+    part = source.shape[0] // 4
+    parts = [pl.ds(n * part, part) for n in range(4)]
+    loads = [pltpu.make_async_copy(source.at[here], held.at[here], in_sem.at[n]) for n, here in enumerate(parts)]
+    stores = [pltpu.make_async_copy(held.at[here], target.at[here], out_sem.at[n]) for n, here in enumerate(parts)]
+    for load in loads:
+        load.start()
+    for load, store in zip(loads, stores):
+        load.wait()
+        store.start()
+    for store in stores:
+        store.wait()
 
 
 def on_device(n_lat, n_lon, concentration, cotangent, coag_rate, weights, departure, send_list):
@@ -392,12 +410,17 @@
     total = pl.pallas_call(
         functools.partial(return_kernel, n_lat, n_lon, cells, cap),
         out_shape=jax.ShapeDtypeStruct((cells, bins), F32),
-        in_specs=[ANY, ANY], out_specs=VMEM,
-        scratch_shapes=[pltpu.VMEM((blocks * cap // bins, bins), I32), pltpu.VMEM((blocks, cap, bins), F32), dma, dma,
+        in_specs=[ANY, ANY], out_specs=ANY,
+        scratch_shapes=[pltpu.VMEM((blocks * cap // bins, bins), I32), pltpu.VMEM((cells, bins), F32),
+                        pltpu.VMEM((blocks, cap, bins), F32), dma, dma, dma,
                         dma((blocks,)), dma((blocks,))],
         compiler_params=pltpu.CompilerParams(
             collective_id=1, has_side_effects=True, vmem_limit_bytes=60 * 2**20),
     )(send_list.reshape(blocks * cap // bins, bins), sums)
+    total = pl.pallas_call(
+        copy_kernel, out_shape=jax.ShapeDtypeStruct((cells, bins), F32), in_specs=[ANY], out_specs=ANY,
+        scratch_shapes=[pltpu.VMEM((cells, bins), F32), dma((4,)), dma((4,))],
+        compiler_params=pltpu.CompilerParams(vmem_limit_bytes=60 * 2**20))(total)
     return total.reshape(levels, lat_cells, lon_cells, bins)
 
 

time: 133 us -> 129 us (0.970)
  local copies, waits for them, and re-layouts: 2.27 us -> 0 us
  Pallas kernels: 131 us -> 129 us
    unnamed x1 -> x0, local copies, waits for them, and re-layouts: 2.27 us -> none
    pallas_call x1, Pallas kernels: 48.1 us -> 45.8 us  [on_device(): pl.pallas_call(functools.partial(send_kernel, n_lat, n_lon, cells, cap),...]
    pallas_call x0 -> x1, Pallas kernels: none -> 1.98 us  [on_device(): pl.pallas_call(copy_kernel, out_shape=jax.ShapeDtypeStruct((cells, bins),...]
    pallas_call x1, Pallas kernels: 47.6 us -> 46 us  [on_device(): pl.pallas_call(functools.partial(return_kernel, n_lat, n_lon, cells, cap)...]
where the time goes in v6:
time: 129 us
  Pallas kernels  129 us (100%)
    pallas_call x1, Pallas kernels, on_device(): pl.pallas_call(functools.partial(return_kernel, n_lat, n_lon, cells, cap)...  46 us
    pallas_call x1, Pallas kernels, on_device(): pl.pallas_call(functools.partial(send_kernel, n_lat, n_lon, cells, cap),...  45.8 us
    pallas_call x1, Pallas kernels, on_device(): pl.pallas_call(functools.partial(cell_kernel, cells, corners), out_shape=...  35.1 us

profile of v6, /device:TPU:17, one launch (start us, length us, event | category | flops | bytes accessed | tf_op | source)
XLA Modules:
  0.0 128.9 jit_solution(1721501936938147021)
XLA Ops:
  0.0 45.8 %shard_map.82 = (f32[10240,128]{1,0:T(8,128)}, f32[16384,128]{1,0:T(8,128)}, s32[128,128]{1,0:T(8,128)}) custom-call(s32[9216]{0:T(1024)} %bitcast.8, f32[2048,128]{1,0:T(8,128)} %bitcast.7, f32[8,8,16,16]{3,2,1,0:T(8,128)} %weights_in.1, s32[8,8,16,16]{3,2,1,0:T(8,128)} %departure_in.1), custom_call_target="tpu_custom_call" | custom-call | tf_op jit(solution)/shard_map/pallas_call | solution.py:381
  45.8 35.1 %shard_map.83.sums = f32[10240,128]{1,0:T(8,128)} custom-call(s32[16384]{0:T(1024)} %bitcast.10, f32[16384,128]{1,0:T(8,128)} %get-tuple-element.9.refs_1_, f32[10240,128]{1,0:T(8,128)} %get-tuple-element.10.refs_2_, f32[2048,128]{1,0:T(8,128)} %bitcast.6, f32[8,16,16]{2,1,0:T(8,128)} %refs_4_.1, bf16[128,256]{1,0:T(8,128)(2,1)} %constant.7.refs_5_, ...), custom_call_target="tpu_custom_call" | custom-call | tf_op jit(solution)/shard_map/pallas_call | solution.py:397
  80.9 46.0 %shard_map.84.source = f32[2048,128]{1,0:T(8,128)} custom-call(s32[72,128]{1,0:T(8,128)} %bitcast.9, f32[10240,128]{1,0:T(8,128)} %shard_map.83.sums), custom_call_target="tpu_custom_call" | custom-call | tf_op jit(solution)/shard_map/pallas_call | solution.py:410
  126.9 2.0 %shard_map.85 = f32[2048,128]{1,0:T(8,128)} custom-call(f32[2048,128]{1,0:T(8,128)} %shard_map.84.source), custom_call_target="tpu_custom_call" | custom-call | tf_op jit(solution)/shard_map/pallas_call | solution.py:420

commit v7 on v6

--- a/solution.py
+++ b/solution.py
@@ -209,12 +209,12 @@
               for n, (source, target) in enumerate(zip(later_in, later))]
     for copy in laters:
         copy.start()
-    step = 16
-    clear = entries * step // cells
+    near = 16
+    clear = entries * near // cells
 
     def gather(i, carry):
-        for j in range(step):
-            a = i * step + j
+        for j in range(near):
+            a = i * near + j
             total = None
             for k in range(corners):
                 row = table[pl.ds(index[k][a], 1), :] * wide[pl.ds(a * corners + k, 1), :]
@@ -226,7 +226,7 @@
 
     def next_part(p, carry):
         wide_copy(p).wait()
-        lax.fori_loop(p * (part // step), (p + 1) * (part // step), gather, 0)
+        lax.fori_loop(p * (part // near), (p + 1) * (part // near), gather, 0)
         return carry
 
     lax.fori_loop(0, PARTS, next_part, 0)
@@ -264,6 +264,7 @@
 
     lax.fori_loop(0, cells // tile, react, 0)
 
+    step = 32
     def scatter(i, carry):
         for j in range(step):
             a = i * step + j
@@ -348,9 +349,11 @@
     keep.start()
     load.wait()
     keep.wait()
-    collect(BACK[6:])
-    sent(BACK[:2])
-    send(BACK[4:6])
+    for n in range(2):
+        collect(BACK[6 + n:7 + n])
+    for n in range(2):
+        sent(BACK[n:n + 1])
+        send(BACK[4 + n:5 + n])
     collect(BACK[:6])
     sent(BACK[2:])
     pltpu.make_async_copy(out, result, out_sem).wait()

time: 129 us -> 129 us (level)
  no operation moved by 1% of the time
where the time goes in v7:
time: 129 us
  Pallas kernels  129 us (100%)
    pallas_call x1, Pallas kernels, on_device(): pl.pallas_call(functools.partial(return_kernel, n_lat, n_lon, cells, cap)...  45.9 us
    pallas_call x1, Pallas kernels, on_device(): pl.pallas_call(functools.partial(send_kernel, n_lat, n_lon, cells, cap),...  45.8 us
    pallas_call x1, Pallas kernels, on_device(): pl.pallas_call(functools.partial(cell_kernel, cells, corners), out_shape=...  34.9 us

profile of v7, /device:TPU:17, one launch (start us, length us, event | category | flops | bytes accessed | tf_op | source)
XLA Modules:
  0.0 128.7 jit_solution(17276935976376561147)
XLA Ops:
  0.0 45.8 %shard_map.82 = (f32[10240,128]{1,0:T(8,128)}, f32[16384,128]{1,0:T(8,128)}, s32[128,128]{1,0:T(8,128)}) custom-call(s32[9216]{0:T(1024)} %bitcast.8, f32[2048,128]{1,0:T(8,128)} %bitcast.7, f32[8,8,16,16]{3,2,1,0:T(8,128)} %weights_in.1, s32[8,8,16,16]{3,2,1,0:T(8,128)} %departure_in.1), custom_call_target="tpu_custom_call" | custom-call | tf_op jit(solution)/shard_map/pallas_call | solution.py:384
  45.8 34.9 %shard_map.83.sums = f32[10240,128]{1,0:T(8,128)} custom-call(s32[16384]{0:T(1024)} %bitcast.10, f32[16384,128]{1,0:T(8,128)} %get-tuple-element.9.refs_1_, f32[10240,128]{1,0:T(8,128)} %get-tuple-element.10.refs_2_, f32[2048,128]{1,0:T(8,128)} %bitcast.6, f32[8,16,16]{2,1,0:T(8,128)} %refs_4_.1, bf16[128,256]{1,0:T(8,128)(2,1)} %constant.7.refs_5_, ...), custom_call_target="tpu_custom_call" | custom-call | tf_op jit(solution)/shard_map/pallas_call | solution.py:400
  80.7 45.9 %shard_map.84.source = f32[2048,128]{1,0:T(8,128)} custom-call(s32[72,128]{1,0:T(8,128)} %bitcast.9, f32[10240,128]{1,0:T(8,128)} %shard_map.83.sums), custom_call_target="tpu_custom_call" | custom-call | tf_op jit(solution)/shard_map/pallas_call | solution.py:413
  126.7 2.0 %shard_map.85 = f32[2048,128]{1,0:T(8,128)} custom-call(f32[2048,128]{1,0:T(8,128)} %shard_map.84.source), custom_call_target="tpu_custom_call" | custom-call | tf_op jit(solution)/shard_map/pallas_call | solution.py:423

commit v8 on v7

--- a/solution.py
+++ b/solution.py
@@ -78,8 +78,8 @@
 
 
 def send_kernel(n_lat, n_lon, cells, cap, slots_in, own_in, weights_in, departure_in, table, spread, named, slots, own,
-                weights, departure, rows, wide, flat, in_sem, own_sem, wide_sem, flat_sem, send_sem, recv_sem, half_send,
-                half_recv):
+                weights, departure, rows, wide, flat, in_sem, own_sem, wide_sem, flat_sem, send_sem, recv_sem, piece_send,
+                piece_recv):
     pairs = ((slots_in, slots), (own_in, own), (weights_in, weights), (departure_in, departure))
     loads = [pltpu.make_async_copy(source, target, in_sem.at[n]) for n, (source, target) in enumerate(pairs)]
     for load in loads:
@@ -96,15 +96,16 @@
             src_ref=rows.at[b], dst_ref=table.at[pl.ds(cells + slot(u, v) * cap, cap)], send_sem=send_sem.at[b],
             recv_sem=recv_sem.at[b], device_id=place.at(2 - u, 2 - v), device_id_type=MESH)
 
-    half = cap // 2
-
-    def half_copy(u, v, h):
+    pieces = 4
+    size = cap // pieces
+
+    def piece_copy(u, v, h):
         b = 3 * u + v
-        sem = 2 * (v // 2) + h
+        sem = pieces * (v // 2) + h
         return pltpu.make_async_remote_copy(
-            src_ref=rows.at[b, pl.ds(h * half, half)],
-            dst_ref=table.at[pl.ds(cells + slot(u, v) * cap + h * half, half)], send_sem=half_send.at[sem],
-            recv_sem=half_recv.at[sem], device_id=place.at(2 - u, 2 - v), device_id_type=MESH)
+            src_ref=rows.at[b, pl.ds(h * size, size)],
+            dst_ref=table.at[pl.ds(cells + slot(u, v) * cap + h * size, size)], send_sem=piece_send.at[sem],
+            recv_sem=piece_recv.at[sem], device_id=place.at(2 - u, 2 - v), device_id_type=MESH)
 
     def pick(b, low, count):
         step = 32
@@ -117,10 +118,10 @@
 
         lax.fori_loop(0, count // step, gather, 0)
 
-    for h in range(2):
+    for h in range(pieces):
         for u, v in FIRST:
-            pick(3 * u + v, h * half, half)
-            half_copy(u, v, h).start()
+            pick(3 * u + v, h * size, size)
+            piece_copy(u, v, h).start()
     for u, v in NEXT:
         @pl.when(place.has(2 - u))
         def _():
@@ -166,10 +167,10 @@
     keep.wait()
     store.wait()
     note.wait()
-    for h in range(2):
+    for h in range(pieces):
         for u, v in FIRST:
-            half_copy(u, v, h).wait_recv()
-            half_copy(u, v, h).wait_send()
+            piece_copy(u, v, h).wait_recv()
+            piece_copy(u, v, h).wait_send()
     for u, v in NEXT:
         @pl.when(place.has(u))
         def _():
@@ -390,7 +391,7 @@
                         pltpu.VMEM(weights.shape, F32), pltpu.VMEM(departure.shape, I32),
                         pltpu.VMEM((blocks, cap, bins), F32), pltpu.VMEM((cells * corners, bins), F32),
                         pltpu.VMEM((corners * cells // bins, bins), I32), dma((4,)), dma, dma, dma, dma((blocks,)), dma((blocks,)),
-                        dma((4,)), dma((4,))],
+                        dma((8,)), dma((8,))],
         compiler_params=pltpu.CompilerParams(
             collective_id=0, has_side_effects=True, vmem_limit_bytes=60 * 2**20),
     )(send_list.reshape(blocks * cap), own, weights, departure)

time: 129 us -> 129 us (level)
  no operation moved by 1% of the time
where the time goes in v8:
time: 129 us; the launch traced here: 128 us
  Pallas kernels  128 us (99%)
    pallas_call x1, Pallas kernels, on_device(): pl.pallas_call(functools.partial(return_kernel, n_lat, n_lon, cells, cap)...  45.7 us
    pallas_call x1, Pallas kernels, on_device(): pl.pallas_call(functools.partial(send_kernel, n_lat, n_lon, cells, cap),...  45.7 us
    pallas_call x1, Pallas kernels, on_device(): pl.pallas_call(functools.partial(cell_kernel, cells, corners), out_shape=...  34.9 us

profile of v8, /device:TPU:17, one launch (start us, length us, event | category | flops | bytes accessed | tf_op | source)
XLA Modules:
  0.0 128.2 jit_solution(10284213585650951304)
XLA Ops:
  0.0 45.7 %shard_map.82 = (f32[10240,128]{1,0:T(8,128)}, f32[16384,128]{1,0:T(8,128)}, s32[128,128]{1,0:T(8,128)}) custom-call(s32[9216]{0:T(1024)} %bitcast.8, f32[2048,128]{1,0:T(8,128)} %bitcast.7, f32[8,8,16,16]{3,2,1,0:T(8,128)} %weights_in.1, s32[8,8,16,16]{3,2,1,0:T(8,128)} %departure_in.1), custom_call_target="tpu_custom_call" | custom-call | tf_op jit(solution)/shard_map/pallas_call | solution.py:385
  45.7 34.9 %shard_map.83.sums = f32[10240,128]{1,0:T(8,128)} custom-call(s32[16384]{0:T(1024)} %bitcast.10, f32[16384,128]{1,0:T(8,128)} %get-tuple-element.9.refs_1_, f32[10240,128]{1,0:T(8,128)} %get-tuple-element.10.refs_2_, f32[2048,128]{1,0:T(8,128)} %bitcast.6, f32[8,16,16]{2,1,0:T(8,128)} %refs_4_.1, bf16[128,256]{1,0:T(8,128)(2,1)} %constant.7.refs_5_, ...), custom_call_target="tpu_custom_call" | custom-call | tf_op jit(solution)/shard_map/pallas_call | solution.py:401
  80.5 45.7 %shard_map.84.source = f32[2048,128]{1,0:T(8,128)} custom-call(s32[72,128]{1,0:T(8,128)} %bitcast.9, f32[10240,128]{1,0:T(8,128)} %shard_map.83.sums), custom_call_target="tpu_custom_call" | custom-call | tf_op jit(solution)/shard_map/pallas_call | solution.py:414
  126.2 2.0 %shard_map.85 = f32[2048,128]{1,0:T(8,128)} custom-call(f32[2048,128]{1,0:T(8,128)} %shard_map.84.source), custom_call_target="tpu_custom_call" | custom-call | tf_op jit(solution)/shard_map/pallas_call | solution.py:424
